TPU v7x, 768 devices: a whole 4x8x12 slice. The times are simulated.
768 devices in a mesh: space: 192 (over y_lo, z, x, core), tm: 4 (over y_hi).
Axes of the slice: x: 4, y: 8 (y_hi: 4, y_lo: 2; y = y_hi * 2 + y_lo), z: 12, core: 2. Of those that a mesh axis runs over, the one named last changes fastest.
Arguments:
- guess_pressure: float32 [4, 384, 64, 128], P('tm', 'space'), may hold values from -6 to 6
- guess_velocity: float32 [4, 3, 384, 64, 128], P('tm', None, 'space'), may hold values from -6 to 6
- initial_pressure: float32 [384, 64, 128], P('space'), may hold values from -6 to 6
- initial_velocity: float32 [3, 384, 64, 128], P(None, 'space'), may hold values from -6 to 6
- stiffness: float32 [384, 64, 128], P('space'), may hold values from 0.5 to 2
- inv_mass: float32 [384, 64, 128], P('space'), may hold values from 0.5 to 2
Outputs:
- corrected_pressure: float32 [4, 384, 64, 128], P('tm', 'space')
- corrected_velocity: float32 [4, 3, 384, 64, 128], P('tm', None, 'space')
- residual_pressure: float32 [4, 384, 64, 128], P('tm', 'space')
- residual_velocity: float32 [4, 3, 384, 64, 128], P('tm', None, 'space')
All inputs are finite; a program needn't handle non-finite values.
Results may differ from a plain program's by a relative error of at most 0.00002.
Values sent between devices are 32-bit elements; how exact they have to be, the bound alone decides.
A program may use at most 32 MiB of HBM per device.

v0:
```python
import jax
import jax.numpy as jnp
from jax import lax
from jax.sharding import PartitionSpec as P

STEPS = 4


DT_COARSE = 0.4


def from_behind(x, axis, by):
    size = lax.axis_size(axis)
    pairs = [(i, i + by) for i in range(size) if 0 <= i + by < size]
    return lax.ppermute(x, axis, pairs)


def neighbour_sum(values, offset, axis):
    return values + jnp.roll(values, offset, axis=axis)


def node_forces(pressure, lower_zones):
    combined = pressure + lower_zones
    force_x = 0.25 * (
        neighbour_sum(neighbour_sum(lower_zones, 1, -1), 1, -2)
        - neighbour_sum(neighbour_sum(pressure, 1, -1), 1, -2)
    )
    across_z = neighbour_sum(combined, 1, -1)
    force_y = 0.25 * (jnp.roll(across_z, 1, axis=-2) - across_z)
    across_y = neighbour_sum(combined, 1, -2)
    force_z = 0.25 * (jnp.roll(across_y, 1, axis=-1) - across_y)
    return jnp.stack([force_x, force_y, force_z])


def zone_divergence(velocity, upper_nodes):
    diff_x = neighbour_sum(neighbour_sum(upper_nodes[0] - velocity[0], -1, -1), -1, -2)
    sum_y = neighbour_sum(velocity[1] + upper_nodes[1], -1, -1)
    diff_y = jnp.roll(sum_y, -1, axis=-2) - sum_y
    sum_z = neighbour_sum(velocity[2] + upper_nodes[2], -1, -2)
    diff_z = jnp.roll(sum_z, -1, axis=-1) - sum_z
    return 0.25 * (diff_x + diff_y + diff_z)


def advance(pressure, velocity, stiffness, inv_mass, step_size):
    empty_plane = jnp.zeros_like(pressure[:1])
    lower_zones = jnp.concatenate([empty_plane, pressure[:-1]], axis=0)
    forces = node_forces(pressure, lower_zones)
    outgoing = node_forces(empty_plane, pressure[-1:])
    incoming = from_behind(outgoing, "space", 1)
    forces = jnp.concatenate([forces[:, :1] + incoming, forces[:, 1:]], axis=1)
    velocity = velocity + step_size * inv_mass * forces
    edge_nodes = from_behind(velocity[:, :1], "space", -1)
    upper_nodes = jnp.concatenate([velocity[:, 1:], edge_nodes], axis=1)
    pressure = pressure - step_size * stiffness * zone_divergence(velocity, upper_nodes)
    return (pressure, velocity)


def propagate(pressure, velocity, stiffness, inv_mass):
    fine_size = DT_COARSE / STEPS
    for repeat in range(STEPS):
        pressure, velocity = advance(pressure, velocity, stiffness, inv_mass, fine_size)
    return (pressure, velocity)


def on_device(
    guess_pressure, guess_velocity, initial_pressure, initial_velocity, stiffness, inv_mass
):
    relaxed_p, relaxed_v = propagate(guess_pressure[0], guess_velocity[0], stiffness, inv_mass)
    shifted_p, shifted_v = from_behind((relaxed_p, relaxed_v), "tm", 1)
    first_group = lax.axis_index("tm") == 0
    second_p = jnp.where(first_group, initial_pressure, shifted_p)
    second_v = jnp.where(first_group, initial_velocity, shifted_v)
    end_p, end_v = propagate(second_p, second_v, stiffness, inv_mass)
    resid_p = end_p - relaxed_p
    resid_v = end_v - relaxed_v
    error_p, error_v = (resid_p, resid_v)
    groups = lax.axis_size("tm")
    carried_p, carried_v = (resid_p, resid_v)
    for repeat in range(groups - 1):
        carried_p, carried_v = from_behind((carried_p, carried_v), "tm", 1)
        carried_p, carried_v = advance(carried_p, carried_v, stiffness, inv_mass, DT_COARSE)
        error_p = error_p + carried_p
        error_v = error_v + carried_v
    corrected_p = relaxed_p + error_p
    corrected_v = relaxed_v + error_v
    return (corrected_p[None], corrected_v[None], resid_p[None], resid_v[None])


def solution(mesh):
    placed = (
        P("tm", "space", None, None),
        P("tm", None, "space", None, None),
        P("space", None, None),
        P(None, "space", None, None),
        P("space", None, None),
        P("space", None, None),
    )
    return jax.shard_map(
        on_device,
        mesh=mesh,
        in_specs=placed,
        out_specs=(
            P("tm", "space", None, None),
            P("tm", None, "space", None, None),
            P("tm", "space", None, None),
            P("tm", None, "space", None, None),
        ),
        check_vma=False,
    )
```

profile of v0, /device:TPU:56, one launch (start us, length us, event | category | flops | bytes accessed | tf_op | source)
XLA Modules:
  0.0 226.5 jit_solution(1237892785084291460)
XLA Ops:
  2.6 1.9 collective-permute-start
  6.1 15.8 %collective-permute-done = f32[3,1,64,128]{3,2,1,0:T(8,128)S(1)} collective-permute-done((f32[3,1,64,128]{3,2,1,0:T(8,128)S(1)}, f32[3,1,64,128]{3,2,1,0:T(8,128)S(1)}, u32[]{:S(2)}, u32[]{:S(2)}) %collective-permute-start) | collective-permute-done | bytes 98336 | tf_op jit(solution)/shard_map/ppermute | solution.py:15
  22.0 2.0 collective-permute-start.1
  24.1 2.2 collective-permute-done.1
  30.8 8.1 %collective-permute-done.2 = f32[3,1,64,128]{3,2,1,0:T(8,128)S(1)} collective-permute-done((f32[3,1,64,128]{3,2,1,0:T(8,128)S(1)}, f32[3,1,64,128]{3,2,1,0:T(8,128)S(1)}, u32[]{:S(2)}, u32[]{:S(2)}) %collective-permute-start.2) | collective-permute-done | bytes 98336 | tf_op jit(solution)/shard_map/ppermute | solution.py:15
  39.0 1.9 collective-permute-start.3
  40.9 2.2 collective-permute-done.3
  46.9 8.1 %collective-permute-done.4 = f32[3,1,64,128]{3,2,1,0:T(8,128)S(1)} collective-permute-done((f32[3,1,64,128]{3,2,1,0:T(8,128)S(1)}, f32[3,1,64,128]{3,2,1,0:T(8,128)S(1)}, u32[]{:S(2)}, u32[]{:S(2)}) %collective-permute-start.4) | collective-permute-done | bytes 98336 | tf_op jit(solution)/shard_map/ppermute | solution.py:15
  57.1 2.2 collective-permute-done.5
  63.0 8.8 %collective-permute-done.6 = f32[3,1,64,128]{3,2,1,0:T(8,128)S(1)} collective-permute-done((f32[3,1,64,128]{3,2,1,0:T(8,128)S(1)}, f32[3,1,64,128]{3,2,1,0:T(8,128)S(1)}, u32[]{:S(2)}, u32[]{:S(2)}) %collective-permute-start.6) | collective-permute-done | bytes 98336 | tf_op jit(solution)/shard_map/ppermute | solution.py:15
  73.9 2.2 collective-permute-done.7
  79.4 5.0 %collective-permute-done.8 = f32[2,64,128]{2,1,0:T(8,128)S(1)} collective-permute-done((f32[2,64,128]{2,1,0:T(8,128)S(1)}, f32[2,64,128]{2,1,0:T(8,128)S(1)}, u32[]{:S(2)}, u32[]{:S(2)}) %collective-permute-start.8) | collective-permute-done | bytes 65568 | tf_op jit(solution)/shard_map/ppermute | solution.py:15
  85.3 1.9 collective-permute-start.10
  87.4 8.0 %collective-permute-done.10 = f32[3,1,64,128]{3,2,1,0:T(8,128)S(1)} collective-permute-done((f32[3,1,64,128]{3,2,1,0:T(8,128)S(1)}, f32[3,1,64,128]{3,2,1,0:T(8,128)S(1)}, u32[]{:S(2)}, u32[]{:S(2)}) %collective-permute-start.10) | collective-permute-done | bytes 98336 | tf_op jit(solution)/shard_map/ppermute | solution.py:15
  95.6 1.9 collective-permute-start.11
  97.5 2.2 collective-permute-done.11
  103.5 8.1 %collective-permute-done.12 = f32[3,1,64,128]{3,2,1,0:T(8,128)S(1)} collective-permute-done((f32[3,1,64,128]{3,2,1,0:T(8,128)S(1)}, f32[3,1,64,128]{3,2,1,0:T(8,128)S(1)}, u32[]{:S(2)}, u32[]{:S(2)}) %collective-permute-start.12) | collective-permute-done | bytes 98336 | tf_op jit(solution)/shard_map/ppermute | solution.py:15
  113.6 2.2 collective-permute-done.13
  119.6 8.1 %collective-permute-done.14 = f32[3,1,64,128]{3,2,1,0:T(8,128)S(1)} collective-permute-done((f32[3,1,64,128]{3,2,1,0:T(8,128)S(1)}, f32[3,1,64,128]{3,2,1,0:T(8,128)S(1)}, u32[]{:S(2)}, u32[]{:S(2)}) %collective-permute-start.14) | collective-permute-done | bytes 98336 | tf_op jit(solution)/shard_map/ppermute | solution.py:15
  129.7 2.2 collective-permute-done.15
  135.7 9.2 %collective-permute-done.16 = f32[3,1,64,128]{3,2,1,0:T(8,128)S(1)} collective-permute-done((f32[3,1,64,128]{3,2,1,0:T(8,128)S(1)}, f32[3,1,64,128]{3,2,1,0:T(8,128)S(1)}, u32[]{:S(2)}, u32[]{:S(2)}) %collective-permute-start.16) | collective-permute-done | bytes 98336 | tf_op jit(solution)/shard_map/ppermute | solution.py:15
  147.0 2.2 collective-permute-done.17
  152.5 5.7 %collective-permute-done.18 = f32[2,64,128]{2,1,0:T(8,128)S(1)} collective-permute-done((f32[2,64,128]{2,1,0:T(8,128)S(1)}, f32[2,64,128]{2,1,0:T(8,128)S(1)}, u32[]{:S(2)}, u32[]{:S(2)}) %collective-permute-start.18) | collective-permute-done | bytes 65568 | tf_op jit(solution)/shard_map/ppermute | solution.py:15
  161.2 9.1 %collective-permute-done.20 = f32[3,1,64,128]{3,2,1,0:T(8,128)S(1)} collective-permute-done((f32[3,1,64,128]{3,2,1,0:T(8,128)S(1)}, f32[3,1,64,128]{3,2,1,0:T(8,128)S(1)}, u32[]{:S(2)}, u32[]{:S(2)}) %collective-permute-start.20) | collective-permute-done | bytes 98336 | tf_op jit(solution)/shard_map/ppermute | solution.py:15
  172.3 2.2 collective-permute-done.21
  177.8 6.3 %collective-permute-done.22 = f32[2,64,128]{2,1,0:T(8,128)S(1)} collective-permute-done((f32[2,64,128]{2,1,0:T(8,128)S(1)}, f32[2,64,128]{2,1,0:T(8,128)S(1)}, u32[]{:S(2)}, u32[]{:S(2)}) %collective-permute-start.22) | collective-permute-done | bytes 65568 | tf_op jit(solution)/shard_map/ppermute | solution.py:15
  185.0 1.9 collective-permute-start.24
  187.1 8.1 %collective-permute-done.24 = f32[3,1,64,128]{3,2,1,0:T(8,128)S(1)} collective-permute-done((f32[3,1,64,128]{3,2,1,0:T(8,128)S(1)}, f32[3,1,64,128]{3,2,1,0:T(8,128)S(1)}, u32[]{:S(2)}, u32[]{:S(2)}) %collective-permute-start.24) | collective-permute-done | bytes 98336 | tf_op jit(solution)/shard_map/ppermute | solution.py:15
  197.2 2.2 collective-permute-done.25
  202.6 6.3 %collective-permute-done.26 = f32[2,64,128]{2,1,0:T(8,128)S(1)} collective-permute-done((f32[2,64,128]{2,1,0:T(8,128)S(1)}, f32[2,64,128]{2,1,0:T(8,128)S(1)}, u32[]{:S(2)}, u32[]{:S(2)}) %collective-permute-start.26) | collective-permute-done | bytes 65568 | tf_op jit(solution)/shard_map/ppermute | solution.py:15
  212.0 8.1 %collective-permute-done.28 = f32[3,1,64,128]{3,2,1,0:T(8,128)S(1)} collective-permute-done((f32[3,1,64,128]{3,2,1,0:T(8,128)S(1)}, f32[3,1,64,128]{3,2,1,0:T(8,128)S(1)}, u32[]{:S(2)}, u32[]{:S(2)}) %collective-permute-start.28) | collective-permute-done | bytes 98336 | tf_op jit(solution)/shard_map/ppermute | solution.py:15
  223.0 2.2 collective-permute-done.29
  (509 shorter events, 64.7 us)
Async XLA Ops:
  2.6 19.3 %collective-permute-start = (f32[3,1,64,128]{3,2,1,0:T(8,128)S(1)}, f32[3,1,64,128]{3,2,1,0:T(8,128)S(1)}, u32[]{:S(2)}, u32[]{:S(2)}) collective-permute-start(f32[3,1,64,128]{3,2,1,0:T(8,128)S(1)} %pad_maximum_fusion.11), channel_id=1, source_target_pairs={{0,4},{4,8},{8,12},{12,16},{16,20},{20,24},{24,28},{28,32},{32,36}... | collective-permute-start | bytes 294920 | tf_op jit(solution)/shard_map/ppermute | solution.py:15
  22.0 4.2 %collective-permute-start.1 = (f32[3,1,64,128]{3,2,1,0:T(8,128)S(1)}, f32[3,1,64,128]{3,2,1,0:T(8,128)S(1)}, u32[]{:S(2)}, u32[]{:S(2)}) collective-permute-start(f32[3,1,64,128]{3,2,1,0:T(8,128)S(1)} %get-tuple-element.81), channel_id=1, source_target_pairs={{4,0},{8,4},{12,8},{16,12},{20,16},{24,20},{28,24},{32,28},{36,32}... | collective-permute-start | bytes 294920 | tf_op jit(solution)/shard_map/ppermute | solution.py:15
  28.7 10.2 %collective-permute-start.2 = (f32[3,1,64,128]{3,2,1,0:T(8,128)S(1)}, f32[3,1,64,128]{3,2,1,0:T(8,128)S(1)}, u32[]{:S(2)}, u32[]{:S(2)}) collective-permute-start(f32[3,1,64,128]{3,2,1,0:T(8,128)S(1)} %pad_maximum_fusion.12), channel_id=1, source_target_pairs={{0,4},{4,8},{8,12},{12,16},{16,20},{20,24},{24,28},{28,32},{32,36}... | collective-permute-start | bytes 294920 | tf_op jit(solution)/shard_map/ppermute | solution.py:15
  39.0 4.1 %collective-permute-start.3 = (f32[3,1,64,128]{3,2,1,0:T(8,128)S(1)}, f32[3,1,64,128]{3,2,1,0:T(8,128)S(1)}, u32[]{:S(2)}, u32[]{:S(2)}) collective-permute-start(f32[3,1,64,128]{3,2,1,0:T(8,128)S(1)} %get-tuple-element.77), channel_id=1, source_target_pairs={{4,0},{8,4},{12,8},{16,12},{20,16},{24,20},{28,24},{32,28},{36,32}... | collective-permute-start | bytes 294920 | tf_op jit(solution)/shard_map/ppermute | solution.py:15
  44.8 10.2 %collective-permute-start.4 = (f32[3,1,64,128]{3,2,1,0:T(8,128)S(1)}, f32[3,1,64,128]{3,2,1,0:T(8,128)S(1)}, u32[]{:S(2)}, u32[]{:S(2)}) collective-permute-start(f32[3,1,64,128]{3,2,1,0:T(8,128)S(1)} %pad_maximum_fusion.13), channel_id=1, source_target_pairs={{0,4},{4,8},{8,12},{12,16},{16,20},{20,24},{24,28},{28,32},{32,36}... | collective-permute-start | bytes 294920 | tf_op jit(solution)/shard_map/ppermute | solution.py:15
  55.1 4.1 %collective-permute-start.5 = (f32[3,1,64,128]{3,2,1,0:T(8,128)S(1)}, f32[3,1,64,128]{3,2,1,0:T(8,128)S(1)}, u32[]{:S(2)}, u32[]{:S(2)}) collective-permute-start(f32[3,1,64,128]{3,2,1,0:T(8,128)S(1)} %get-tuple-element.73), channel_id=1, source_target_pairs={{4,0},{8,4},{12,8},{16,12},{20,16},{24,20},{28,24},{32,28},{36,32}... | collective-permute-start | bytes 294920 | tf_op jit(solution)/shard_map/ppermute | solution.py:15
  60.9 10.9 %collective-permute-start.6 = (f32[3,1,64,128]{3,2,1,0:T(8,128)S(1)}, f32[3,1,64,128]{3,2,1,0:T(8,128)S(1)}, u32[]{:S(2)}, u32[]{:S(2)}) collective-permute-start(f32[3,1,64,128]{3,2,1,0:T(8,128)S(1)} %pad_maximum_fusion.14), channel_id=1, source_target_pairs={{0,4},{4,8},{8,12},{12,16},{16,20},{20,24},{24,28},{28,32},{32,36}... | collective-permute-start | bytes 294920 | tf_op jit(solution)/shard_map/ppermute | solution.py:15
  72.0 4.1 %collective-permute-start.7 = (f32[3,1,64,128]{3,2,1,0:T(8,128)S(1)}, f32[3,1,64,128]{3,2,1,0:T(8,128)S(1)}, u32[]{:S(2)}, u32[]{:S(2)}) collective-permute-start(f32[3,1,64,128]{3,2,1,0:T(8,128)S(1)} %get-tuple-element.69), channel_id=1, source_target_pairs={{4,0},{8,4},{12,8},{16,12},{20,16},{24,20},{28,24},{32,28},{36,32}... | collective-permute-start | bytes 294920 | tf_op jit(solution)/shard_map/ppermute | solution.py:15
  76.8 7.6 %collective-permute-start.8 = (f32[2,64,128]{2,1,0:T(8,128)S(1)}, f32[2,64,128]{2,1,0:T(8,128)S(1)}, u32[]{:S(2)}, u32[]{:S(2)}) collective-permute-start(f32[2,64,128]{2,1,0:T(8,128)S(1)} %fusion.146), channel_id=1, source_target_pairs={{0,1},{1,2},{2,3},{4,5},{5,6},{6,7},{8,9},{9,10},{10,11},{12,13},{... | collective-permute-start | bytes 196616 | tf_op jit(solution)/shard_map/ppermute | solution.py:15
  78.1 17.4 %collective-permute-start.9 = (f32[3,2,64,128]{3,2,1,0:T(8,128)S(1)}, f32[3,2,64,128]{3,2,1,0:T(8,128)S(1)}, u32[]{:S(2)}, u32[]{:S(2)}) collective-permute-start(f32[3,2,64,128]{3,2,1,0:T(8,128)S(1)} %fusion.3), channel_id=1, source_target_pairs={{0,1},{1,2},{2,3},{4,5},{5,6},{6,7},{8,9},{9,10},{10,11},{12,13},{... | collective-permute-start | bytes 589832 | tf_op jit(solution)/shard_map/ppermute | solution.py:15
  85.3 10.2 %collective-permute-start.10 = (f32[3,1,64,128]{3,2,1,0:T(8,128)S(1)}, f32[3,1,64,128]{3,2,1,0:T(8,128)S(1)}, u32[]{:S(2)}, u32[]{:S(2)}) collective-permute-start(f32[3,1,64,128]{3,2,1,0:T(8,128)S(1)} %pad_maximum_fusion.15), channel_id=1, source_target_pairs={{0,4},{4,8},{8,12},{12,16},{16,20},{20,24},{24,28},{28,32},{32,36}... | collective-permute-start | bytes 294920 | tf_op jit(solution)/shard_map/ppermute | solution.py:15
  95.6 4.1 %collective-permute-start.11 = (f32[3,1,64,128]{3,2,1,0:T(8,128)S(1)}, f32[3,1,64,128]{3,2,1,0:T(8,128)S(1)}, u32[]{:S(2)}, u32[]{:S(2)}) collective-permute-start(f32[3,1,64,128]{3,2,1,0:T(8,128)S(1)} %get-tuple-element.65), channel_id=1, source_target_pairs={{4,0},{8,4},{12,8},{16,12},{20,16},{24,20},{28,24},{32,28},{36,32}... | collective-permute-start | bytes 294920 | tf_op jit(solution)/shard_map/ppermute | solution.py:15
  101.4 10.2 %collective-permute-start.12 = (f32[3,1,64,128]{3,2,1,0:T(8,128)S(1)}, f32[3,1,64,128]{3,2,1,0:T(8,128)S(1)}, u32[]{:S(2)}, u32[]{:S(2)}) collective-permute-start(f32[3,1,64,128]{3,2,1,0:T(8,128)S(1)} %pad_maximum_fusion.16), channel_id=1, source_target_pairs={{0,4},{4,8},{8,12},{12,16},{16,20},{20,24},{24,28},{28,32},{32,36}... | collective-permute-start | bytes 294920 | tf_op jit(solution)/shard_map/ppermute | solution.py:15
  111.7 4.1 %collective-permute-start.13 = (f32[3,1,64,128]{3,2,1,0:T(8,128)S(1)}, f32[3,1,64,128]{3,2,1,0:T(8,128)S(1)}, u32[]{:S(2)}, u32[]{:S(2)}) collective-permute-start(f32[3,1,64,128]{3,2,1,0:T(8,128)S(1)} %get-tuple-element.61), channel_id=1, source_target_pairs={{4,0},{8,4},{12,8},{16,12},{20,16},{24,20},{28,24},{32,28},{36,32}... | collective-permute-start | bytes 294920 | tf_op jit(solution)/shard_map/ppermute | solution.py:15
  117.5 10.2 %collective-permute-start.14 = (f32[3,1,64,128]{3,2,1,0:T(8,128)S(1)}, f32[3,1,64,128]{3,2,1,0:T(8,128)S(1)}, u32[]{:S(2)}, u32[]{:S(2)}) collective-permute-start(f32[3,1,64,128]{3,2,1,0:T(8,128)S(1)} %pad_maximum_fusion.17), channel_id=1, source_target_pairs={{0,4},{4,8},{8,12},{12,16},{16,20},{20,24},{24,28},{28,32},{32,36}... | collective-permute-start | bytes 294920 | tf_op jit(solution)/shard_map/ppermute | solution.py:15
  127.8 4.1 %collective-permute-start.15 = (f32[3,1,64,128]{3,2,1,0:T(8,128)S(1)}, f32[3,1,64,128]{3,2,1,0:T(8,128)S(1)}, u32[]{:S(2)}, u32[]{:S(2)}) collective-permute-start(f32[3,1,64,128]{3,2,1,0:T(8,128)S(1)} %get-tuple-element.57), channel_id=1, source_target_pairs={{4,0},{8,4},{12,8},{16,12},{20,16},{24,20},{28,24},{32,28},{36,32}... | collective-permute-start | bytes 294920 | tf_op jit(solution)/shard_map/ppermute | solution.py:15
  133.6 11.3 %collective-permute-start.16 = (f32[3,1,64,128]{3,2,1,0:T(8,128)S(1)}, f32[3,1,64,128]{3,2,1,0:T(8,128)S(1)}, u32[]{:S(2)}, u32[]{:S(2)}) collective-permute-start(f32[3,1,64,128]{3,2,1,0:T(8,128)S(1)} %pad_maximum_fusion.18), channel_id=1, source_target_pairs={{0,4},{4,8},{8,12},{12,16},{16,20},{20,24},{24,28},{28,32},{32,36}... | collective-permute-start | bytes 294920 | tf_op jit(solution)/shard_map/ppermute | solution.py:15
  145.0 75.1 %copy-start.3 = (f32[3,2,64,128]{3,2,1,0:T(8,128)}, f32[3,2,64,128]{3,2,1,0:T(8,128)S(1)}, u32[]{:S(2)}) copy-start(f32[3,2,64,128]{3,2,1,0:T(8,128)S(1)} %get-tuple-element.6) | copy-start | bytes 589828
  145.1 4.1 %collective-permute-start.17 = (f32[3,1,64,128]{3,2,1,0:T(8,128)S(1)}, f32[3,1,64,128]{3,2,1,0:T(8,128)S(1)}, u32[]{:S(2)}, u32[]{:S(2)}) collective-permute-start(f32[3,1,64,128]{3,2,1,0:T(8,128)S(1)} %get-tuple-element.53), channel_id=1, source_target_pairs={{4,0},{8,4},{12,8},{16,12},{20,16},{24,20},{28,24},{32,28},{36,32}... | collective-permute-start | bytes 294920 | tf_op jit(solution)/shard_map/ppermute | solution.py:15
  149.9 75.9 %copy-start.4 = (f32[2,64,128]{2,1,0:T(8,128)}, f32[2,64,128]{2,1,0:T(8,128)S(1)}, u32[]{:S(2)}) copy-start(f32[2,64,128]{2,1,0:T(8,128)S(1)} %fusion.195) | copy-start | bytes 196612
  149.9 8.3 %collective-permute-start.18 = (f32[2,64,128]{2,1,0:T(8,128)S(1)}, f32[2,64,128]{2,1,0:T(8,128)S(1)}, u32[]{:S(2)}, u32[]{:S(2)}) collective-permute-start(f32[2,64,128]{2,1,0:T(8,128)S(1)} %fusion.195), channel_id=1, source_target_pairs={{0,1},{1,2},{2,3},{4,5},{5,6},{6,7},{8,9},{9,10},{10,11},{12,13},{... | collective-permute-start | bytes 196616 | tf_op jit(solution)/shard_map/ppermute | solution.py:15
  151.2 19.1 %collective-permute-start.19 = (f32[3,2,64,128]{3,2,1,0:T(8,128)S(1)}, f32[3,2,64,128]{3,2,1,0:T(8,128)S(1)}, u32[]{:S(2)}, u32[]{:S(2)}) collective-permute-start(f32[3,2,64,128]{3,2,1,0:T(8,128)S(1)} %get-tuple-element.6), channel_id=1, source_target_pairs={{0,1},{1,2},{2,3},{4,5},{5,6},{6,7},{8,9},{9,10},{10,11},{12,13},{... | collective-permute-start | bytes 589832 | tf_op jit(solution)/shard_map/ppermute | solution.py:15
  159.1 11.2 %collective-permute-start.20 = (f32[3,1,64,128]{3,2,1,0:T(8,128)S(1)}, f32[3,1,64,128]{3,2,1,0:T(8,128)S(1)}, u32[]{:S(2)}, u32[]{:S(2)}) collective-permute-start(f32[3,1,64,128]{3,2,1,0:T(8,128)S(1)} %pad_maximum_fusion.19), channel_id=1, source_target_pairs={{0,4},{4,8},{8,12},{12,16},{16,20},{20,24},{24,28},{28,32},{32,36}... | collective-permute-start | bytes 294920 | tf_op jit(solution)/shard_map/ppermute | solution.py:15
  170.4 4.1 %collective-permute-start.21 = (f32[3,1,64,128]{3,2,1,0:T(8,128)S(1)}, f32[3,1,64,128]{3,2,1,0:T(8,128)S(1)}, u32[]{:S(2)}, u32[]{:S(2)}) collective-permute-start(f32[3,1,64,128]{3,2,1,0:T(8,128)S(1)} %get-tuple-element.49), channel_id=1, source_target_pairs={{4,0},{8,4},{12,8},{16,12},{20,16},{24,20},{28,24},{32,28},{36,32}... | collective-permute-start | bytes 294920 | tf_op jit(solution)/shard_map/ppermute | solution.py:15
  175.2 8.9 %collective-permute-start.22 = (f32[2,64,128]{2,1,0:T(8,128)S(1)}, f32[2,64,128]{2,1,0:T(8,128)S(1)}, u32[]{:S(2)}, u32[]{:S(2)}) collective-permute-start(f32[2,64,128]{2,1,0:T(8,128)S(1)} %fusion.207), channel_id=1, source_target_pairs={{0,1},{1,2},{2,3},{4,5},{5,6},{6,7},{8,9},{9,10},{10,11},{12,13},{... | collective-permute-start | bytes 196616 | tf_op jit(solution)/shard_map/ppermute | solution.py:15
  176.5 18.7 %collective-permute-start.23 = (f32[3,2,64,128]{3,2,1,0:T(8,128)S(1)}, f32[3,2,64,128]{3,2,1,0:T(8,128)S(1)}, u32[]{:S(2)}, u32[]{:S(2)}) collective-permute-start(f32[3,2,64,128]{3,2,1,0:T(8,128)S(1)} %fusion.8), channel_id=1, source_target_pairs={{0,1},{1,2},{2,3},{4,5},{5,6},{6,7},{8,9},{9,10},{10,11},{12,13},{... | collective-permute-start | bytes 589832 | tf_op jit(solution)/shard_map/ppermute | solution.py:15
  185.0 10.2 %collective-permute-start.24 = (f32[3,1,64,128]{3,2,1,0:T(8,128)S(1)}, f32[3,1,64,128]{3,2,1,0:T(8,128)S(1)}, u32[]{:S(2)}, u32[]{:S(2)}) collective-permute-start(f32[3,1,64,128]{3,2,1,0:T(8,128)S(1)} %pad_maximum_fusion.20), channel_id=1, source_target_pairs={{0,4},{4,8},{8,12},{12,16},{16,20},{20,24},{24,28},{28,32},{32,36}... | collective-permute-start | bytes 294920 | tf_op jit(solution)/shard_map/ppermute | solution.py:15
  195.2 4.1 %collective-permute-start.25 = (f32[3,1,64,128]{3,2,1,0:T(8,128)S(1)}, f32[3,1,64,128]{3,2,1,0:T(8,128)S(1)}, u32[]{:S(2)}, u32[]{:S(2)}) collective-permute-start(f32[3,1,64,128]{3,2,1,0:T(8,128)S(1)} %get-tuple-element.45), channel_id=1, source_target_pairs={{4,0},{8,4},{12,8},{16,12},{20,16},{24,20},{28,24},{32,28},{36,32}... | collective-permute-start | bytes 294920 | tf_op jit(solution)/shard_map/ppermute | solution.py:15
  200.0 8.9 %collective-permute-start.26 = (f32[2,64,128]{2,1,0:T(8,128)S(1)}, f32[2,64,128]{2,1,0:T(8,128)S(1)}, u32[]{:S(2)}, u32[]{:S(2)}) collective-permute-start(f32[2,64,128]{2,1,0:T(8,128)S(1)} %fusion.219), channel_id=1, source_target_pairs={{0,1},{1,2},{2,3},{4,5},{5,6},{6,7},{8,9},{9,10},{10,11},{12,13},{... | collective-permute-start | bytes 196616 | tf_op jit(solution)/shard_map/ppermute | solution.py:15
  201.3 18.7 %collective-permute-start.27 = (f32[3,2,64,128]{3,2,1,0:T(8,128)S(1)}, f32[3,2,64,128]{3,2,1,0:T(8,128)S(1)}, u32[]{:S(2)}, u32[]{:S(2)}) collective-permute-start(f32[3,2,64,128]{3,2,1,0:T(8,128)S(1)} %fusion.9), channel_id=1, source_target_pairs={{0,1},{1,2},{2,3},{4,5},{5,6},{6,7},{8,9},{9,10},{10,11},{12,13},{... | collective-permute-start | bytes 589832 | tf_op jit(solution)/shard_map/ppermute | solution.py:15
  209.9 10.2 %collective-permute-start.28 = (f32[3,1,64,128]{3,2,1,0:T(8,128)S(1)}, f32[3,1,64,128]{3,2,1,0:T(8,128)S(1)}, u32[]{:S(2)}, u32[]{:S(2)}) collective-permute-start(f32[3,1,64,128]{3,2,1,0:T(8,128)S(1)} %pad_maximum_fusion.21), channel_id=1, source_target_pairs={{0,4},{4,8},{8,12},{12,16},{16,20},{20,24},{24,28},{28,32},{32,36}... | collective-permute-start | bytes 294920 | tf_op jit(solution)/shard_map/ppermute | solution.py:15
  221.0 4.1 %collective-permute-start.29 = (f32[3,1,64,128]{3,2,1,0:T(8,128)S(1)}, f32[3,1,64,128]{3,2,1,0:T(8,128)S(1)}, u32[]{:S(2)}, u32[]{:S(2)}) collective-permute-start(f32[3,1,64,128]{3,2,1,0:T(8,128)S(1)} %get-tuple-element.41), channel_id=1, source_target_pairs={{4,0},{8,4},{12,8},{16,12},{20,16},{24,20},{28,24},{32,28},{36,32}... | collective-permute-start | bytes 294920 | tf_op jit(solution)/shard_map/ppermute | solution.py:15
  (6 other events, 34.2 us)
where the time goes:
time: 230 us; the launch traced here: 226 us
  waiting for transfers between devices  147 us (64%)
  starting transfers between devices  52.7 us (23%)
  other arithmetic  12 us (5%)
  local copies, waits for them, and re-layouts  11.7 us (5%)
  between operations  3.14 us (1%)
    ppermute x30, waiting for transfers between devices, from_behind(): return lax.ppermute(x, axis, pairs)  147 us
    ppermute x30, starting transfers between devices, from_behind(): return lax.ppermute(x, axis, pairs)  52.7 us
    slice x193, local copies, waits for them, and re-layouts, neighbour_sum(): return values + jnp.roll(values, offset, axis=axis)  5.54 us
    add x66, other arithmetic, neighbour_sum(): return values + jnp.roll(values, offset, axis=axis)  5.4 us
  transfers between devices with their start and end apart: 30, of which 26 were waited for; matrix products, arithmetic and copies ran while one was open for 3% of the time, Pallas kernels for 0%

commit v1 on v0

v1 whole, which is shorter than its diff:
```python
import functools

import jax
import jax.numpy as jnp
from jax import lax
from jax.experimental import pallas as pl
from jax.experimental.pallas import tpu as pltpu
from jax.sharding import PartitionSpec as P

FINE = 0.4 / 4
COARSE = 0.4
NY, NZ = 64, 128
MESH = pl.DeviceIdType.MESH
SPACE, TM = "space", "tm"
(STATIC, SPREAD, INITIAL, FINE1, FINE2, FINE3, LATE, FIRST1, FIRST2, FIRST3) = range(10)
(GUESS, EARLY, SUMS, LAST, ONCE, TWICE) = range(6)
(MASS, STIFF, RATE, BEFORE, TOTAL, FUTURE, START, RELAXED, RATE0, RATE1, BEFORE1, TOTAL1, BASE_P, BASE_X) = range(14)

SPACE_MESSAGES = {
    STATIC: (4, 5),
    SPREAD: (1, 2),
    INITIAL: (3, 4),
    FINE1: (2, 2),
    FINE2: (2, 2),
    FINE3: (2, 2),
    LATE: (2, 2),
    FIRST1: (2, 2),
    FIRST2: (2, 2),
    FIRST3: (1, 1),
}
GROUP_MESSAGES = {
    GUESS: (6, 1),
    EARLY: (5, 1),
    SUMS: (3, 1),
    LAST: (2, 1),
    ONCE: (5, 2),
    TWICE: (5, 3),
}
KEPT = {
    MASS: 5,
    STIFF: 4,
    RATE: 4,
    BEFORE: 2,
    TOTAL: 4,
    FUTURE: 4,
    START: 3,
    RELAXED: 2,
    RATE0: 4,
    RATE1: 4,
    BEFORE1: 2,
    TOTAL1: 4,
    BASE_P: 2,
    BASE_X: 3,
}


def lower_y(x):
    return pltpu.roll(x, 1, 0)


def upper_y(x):
    return pltpu.roll(x, NY - 1, 0)


def lower_z(x):
    return pltpu.roll(x, 1, 1)


def upper_z(x):
    return pltpu.roll(x, NZ - 1, 1)


def corner_forces(zones):
    parts = []
    for x in zones:
        below = lower_z(x)
        s = below + x
        t = 0.5 * (below - x)
        parts.append((s, lower_y(s), t + lower_y(t)))
    forces = []
    for (s0, r0, t0), (s1, r1, t1) in zip(parts[:-1], parts[1:]):
        forces.append((r0 - s1, s0 - r1, t0 + t1))
    return forces


def gather(less, plus, along):
    a = less + upper_y(plus)
    b = along + upper_y(along)
    return (a - b) + upper_z(a + b)


def curve(zones, mass, stiff):
    weighted = [
        (m * a, m * b, m * c) for (a, b, c), m in zip(corner_forces(zones), mass)
    ]
    out = []
    for (a0, b0, c0), (a1, b1, c1), k in zip(weighted[:-1], weighted[1:], stiff):
        out.append(k * gather(b1 - a0, a1 - b0, c0 + c1))
    return out


def spread_up(v):
    return gather(v[0] - v[1], v[0] + v[1], v[2])


def spread_down(v):
    return gather(-v[0] - v[1], v[1] - v[0], v[2])


def kernel(gp_far, gv_far, ip_far, iv_far, k_far, m_far, *rest):
    far_out, bufs = rest[:4], list(rest[4:])
    space = {}
    for name in SPACE_MESSAGES:
        space[name] = tuple(bufs.pop(0) for _ in range(4))
    group = {}
    for name in GROUP_MESSAGES:
        group[name] = tuple(bufs.pop(0) for _ in range(2))
    kept = {name: bufs.pop(0) for name in KEPT}
    near = bufs[:6]
    gp, gv, ip, iv, stiffness, inv_mass = near
    near_out = bufs[6:10]
    out_cp, out_cv, out_rp, out_rv = near_out
    space_sems, group_sems, near_sems, out_sems = bufs[10:]

    fetched = {}
    far = (gp_far, gv_far, ip_far, iv_far, k_far, m_far)
    for i in (0, 4, 5, 1, 2, 3):
        fetched[i] = pltpu.make_async_copy(far[i], near[i], near_sems.at[i])
        fetched[i].start()

    s, t = lax.axis_index(SPACE), lax.axis_index(TM)
    n_s, n_t = lax.axis_size(SPACE), lax.axis_size(TM)
    has_left, has_right = s > 0, s < n_s - 1

    def space_copy(name, right):
        i = name
        to_right, from_left, to_left, from_right = space[name]
        return pltpu.make_async_remote_copy(
            src_ref=to_right if right else to_left,
            dst_ref=from_left if right else from_right,
            send_sem=space_sems.at[i, 0 if right else 1],
            recv_sem=space_sems.at[i, 2 if right else 3],
            device_id={SPACE: s + 1 if right else s - 1},
            device_id_type=MESH,
        )

    def space_send(name):
        pl.when(has_right)(lambda: space_copy(name, True).start())
        pl.when(has_left)(lambda: space_copy(name, False).start())

    def space_wait(name):
        pl.when(has_left)(lambda: space_copy(name, True).wait_recv())
        pl.when(has_right)(lambda: space_copy(name, False).wait_recv())

    def group_copy(name):
        i = name
        ahead = GROUP_MESSAGES[name][1]
        return pltpu.make_async_remote_copy(
            src_ref=group[name][0] if name != GUESS else gv,
            dst_ref=group[name][1],
            send_sem=group_sems.at[i, 0],
            recv_sem=group_sems.at[i, 1],
            device_id={TM: t + ahead},
            device_id_type=MESH,
        )

    def group_send(name):
        pl.when(t + GROUP_MESSAGES[name][1] < n_t)(lambda: group_copy(name).start())

    def group_wait(name):
        pl.when(t >= GROUP_MESSAGES[name][1])(lambda: group_copy(name).wait_recv())

    barrier = pltpu.get_barrier_semaphore()

    def tell(**where):
        pl.semaphore_signal(barrier, inc=1, device_id=where, device_id_type=MESH)

    pl.when(has_right)(lambda: tell(space=s + 1))
    pl.when(has_left)(lambda: tell(space=s - 1))
    for back in range(1, 4):
        pl.when(t >= back)(lambda back=back: tell(tm=t - back))

    def put(ref, planes):
        for i, x in enumerate(planes):
            ref[i] = x

    def get(ref):
        return [ref[i] for i in range(ref.shape[0])]

    nothing = jnp.zeros((NY, NZ), jnp.float32)

    @pl.when(s == 0)
    def _():
        for name in SPACE_MESSAGES:
            ref = space[name][1]
            put(ref, [nothing] * ref.shape[0])

    @pl.when(s == n_s - 1)
    def _():
        for name in SPACE_MESSAGES:
            ref = space[name][3]
            put(ref, [nothing] * ref.shape[0])

    for name in (ONCE, TWICE):

        @pl.when(t < GROUP_MESSAGES[name][1])
        def _(name=name):
            put(group[name][1], [nothing] * 5)

    for i in (0, 4, 5):
        fetched[i].wait()
    put(space[STATIC][0], [gp[0, 0], gp[0, 1], stiffness[1], inv_mass[1]])
    put(space[STATIC][2], [gp[0, 0], gp[0, 1], stiffness[0], inv_mass[0], inv_mass[1]])

    peers = has_right.astype(jnp.int32) + has_left.astype(jnp.int32) + (n_t - 1 - t)
    pl.semaphore_wait(barrier, peers)

    space_send(STATIC)
    fetched[1].wait()
    v0 = [gv[0, i, 0] for i in range(3)]
    v1 = [gv[0, i, 1] for i in range(3)]
    guess_up, guess_d0 = spread_up(v0), spread_up(v1) + spread_down(v0)
    guess_d1 = spread_down(v1)
    put(space[SPREAD][0], [guess_d1])
    put(space[SPREAD][2], [guess_up, guess_d0])
    space_send(SPREAD)
    fetched[2].wait()
    fetched[3].wait()
    v0 = [iv[i, 0] for i in range(3)]
    v1 = [iv[i, 1] for i in range(3)]
    first_up, first_d0 = spread_up(v0), spread_up(v1) + spread_down(v0)
    first_d1 = spread_down(v1)
    put(space[INITIAL][0], [ip[0], ip[1], first_d1])
    put(space[INITIAL][2], [ip[0], ip[1], first_up, first_d0])
    space_send(INITIAL)
    group_send(GUESS)

    def mass():
        return get(kept[MASS])

    def stiff(scale=None):
        return get(kept[STIFF])

    def fine_pair(zones, rate):
        m, k = mass(), stiff()
        rate = [r - c for r, c in zip(rate, curve(zones, m, k))]
        p1 = [x + r for x, r in zip(zones[1:-1], rate)]
        rate2 = [r - c for r, c in zip(rate[1:3], curve(p1, m[1:4], k[1:3]))]
        p2 = [x + r for x, r in zip(p1[1:3], rate2)]
        return p1, rate, p2, rate2

    def zones_of(name, own):
        left, right = get(space[name][1]), get(space[name][3])
        return left[:2] + own + right[:2]

    def next_rate(zones, before, own):
        return [zones[1] - before[0], own[0], own[1], zones[4] - before[1]]

    space_wait(STATIC)
    left, right = get(space[STATIC][1]), get(space[STATIC][3])
    put(kept[MASS], [left[3], inv_mass[0], inv_mass[1], right[3], right[4]])
    scale = 0.125 * FINE * FINE
    raw = [left[2], stiffness[0], stiffness[1], right[2]]
    put(kept[STIFF], [scale * k for k in raw])
    zones = left[:2] + [gp[0, 0], gp[0, 1]] + right[:2]
    space_wait(SPREAD)
    left, right = get(space[SPREAD][1]), get(space[SPREAD][3])
    spread = [left[0] + guess_up, guess_d0, guess_d1 + right[0], right[1]]
    rate = [(-0.25 * FINE) * k * d for k, d in zip(raw, spread)]
    p1, rate1, p2, rate2 = fine_pair(zones, rate)
    put(space[FINE1][0], p2)
    put(space[FINE1][2], p2)
    space_send(FINE1)
    put(kept[RATE], [rate2[0], rate2[0], rate2[1], rate2[1]])
    put(kept[BEFORE], [p1[0], p1[3]])
    put(kept[TOTAL], [x + y for x, y in zip(zones[1:5], p1)])

    space_wait(INITIAL)
    left, right = get(space[INITIAL][1]), get(space[INITIAL][3])
    zones = left[:2] + [ip[0], ip[1]] + right[:2]
    raw = [k * (-0.25 * FINE / scale) for k in stiff()]
    spread = [left[2] + first_up, first_d0, first_d1 + right[2], right[3]]
    rate = [k * d for k, d in zip(raw, spread)]
    put(kept[RATE0], rate)
    p1, rate1, p2, rate2 = fine_pair(zones, rate)
    put(space[FIRST1][0], p2)
    put(space[FIRST1][2], p2)
    space_send(FIRST1)
    put(kept[RATE1], [rate2[0], rate2[0], rate2[1], rate2[1]])
    put(kept[BEFORE1], [p1[0], p1[3]])
    put(kept[TOTAL1], [x + y for x, y in zip(zones[1:5], p1)])

    space_wait(FINE1)
    zones = zones_of(FINE1, get(space[FINE1][0]))
    old = get(kept[RATE])
    rate = next_rate(zones, get(kept[BEFORE]), [old[1], old[2]])
    p1, rate1, p2, rate2 = fine_pair(zones, rate)
    put(space[FINE2][0], p2)
    put(space[FINE2][2], p2)
    space_send(FINE2)
    put(kept[RATE], [rate2[0], rate2[0], rate2[1], rate2[1]])
    put(kept[BEFORE], [p1[0], p1[3]])
    total = [x + y + z for x, y, z in zip(get(kept[TOTAL]), zones[1:5], p1)]
    put(kept[TOTAL], total)
    put(kept[START], total[:3])
    put(kept[RELAXED], p2)

    space_wait(FIRST1)
    zones = zones_of(FIRST1, get(space[FIRST1][0]))
    old = get(kept[RATE1])
    rate = next_rate(zones, get(kept[BEFORE1]), [old[1], old[2]])
    p1, rate1, p2, rate2 = fine_pair(zones, rate)
    total1 = [x + y + z for x, y, z in zip(get(kept[TOTAL1]), zones[1:5], p1)]
    put(kept[TOTAL1], [0.25 * x for x in total1])
    moved = [p2[0] + 0.25 * total1[1], p2[1] + 0.25 * total1[2]]
    put(space[FIRST2][0], moved)
    put(space[FIRST2][2], moved)
    space_send(FIRST2)

    @pl.when(t == 0)
    def _():
        put(kept[BASE_P], p2)
        put(kept[BASE_X], [0.25 * x for x in total1[:3]])
        put(group[EARLY][1], [-p2[0], -p2[1]] + total1[:3])
        put(group[SUMS][1], [nothing] * 3)
        put(group[LAST][1], p2)
        for i in range(3):
            for j in range(2):
                group[GUESS][1][0, i, j] = iv[i, j]

    put(kept[BEFORE1], p2)

    space_wait(FINE2)
    zones = zones_of(FINE2, get(space[FINE2][0]))
    old = get(kept[RATE])
    rate = next_rate(zones, get(kept[BEFORE]), [old[1], old[2]])
    p1, rate1, p2, rate2 = fine_pair(zones, rate)
    put(space[FINE3][0], p2)
    put(space[FINE3][2], p2)
    space_send(FINE3)
    ahead = [12.0 * rate[i] - 16.0 * rate1[i] - zones[i + 1] for i in (1, 2)]
    sums = [x + 4.0 * y for x, y in zip(get(kept[START]), zones[1:4])]
    put(group[EARLY][0], ahead + sums)
    group_send(EARLY)
    put(kept[FUTURE], ahead + ahead)
    put(kept[RATE], [rate2[0], rate2[0], rate2[1], rate2[1]])
    put(kept[BEFORE], [p1[0], p1[3]])
    put(kept[TOTAL], [0.25 * (y - 3.0 * x) for x, y in zip(zones[1:5], p1)])

    def coarse_pair(zones, value, source):
        m, k = mass(), [16.0 * x for x in stiff()]
        one = [x - c for x, c in zip(value, curve(zones, m, k))]
        if source is not None:
            one = [x + y for x, y in zip(one, source)]
        sums = [x + y for x, y in zip(zones[1:5], one)]
        two = [x - c for x, c in zip(one[1:3], curve(sums, m[1:4], k[1:3]))]
        if source is not None:
            two = [x + y for x, y in zip(two, source[1:3])]
        return one, sums, two

    space_wait(FIRST2)
    zones = zones_of(FIRST2, get(space[FIRST2][0]))
    x0, own = get(kept[TOTAL1]), get(kept[BEFORE1])
    value = [zones[1] - x0[0], own[0], own[1], zones[4] - x0[3]]
    source = [4.0 * x for x in get(kept[RATE0])]
    one, sums, two = coarse_pair(zones, value, source)
    third = [sums[1] + two[0], sums[2] + two[1]]
    put(space[FIRST3][0], [third[1]])
    put(space[FIRST3][2], [third[0]])
    space_send(FIRST3)

    @pl.when(t == 1)
    def _():
        put(kept[BASE_P], one[1:3])
        put(kept[BASE_X], zones[1:4])

    @pl.when(t == 2)
    def _():
        put(kept[BASE_P], two)
        put(kept[BASE_X], sums[:3])

    put(kept[BEFORE1], two)
    put(kept[RATE1], third + third)

    space_wait(FINE3)
    zones = zones_of(FINE3, get(space[FINE3][0]))
    old = get(kept[RATE])
    rate = next_rate(zones, get(kept[BEFORE]), [old[1], old[2]])
    p1, rate1, p2, rate2 = fine_pair(zones, rate)
    total = [x + 0.25 * (y + z) for x, y, z in zip(get(kept[TOTAL]), zones[1:5], p1)]
    ahead = get(kept[FUTURE])
    moved = [total[i + 1] + p2[i] + ahead[i] for i in (0, 1)]
    put(space[LATE][0], moved)
    put(space[LATE][2], moved)
    space_send(LATE)
    put(group[SUMS][0], total[:3])
    group_send(SUMS)
    put(group[LAST][0], p2)
    group_send(LAST)
    put(kept[TOTAL], total)
    put(kept[BEFORE], [p2[0] + ahead[0], p2[1] + ahead[1]])

    space_wait(FIRST3)

    @pl.when(t == 3)
    def _():
        left, right = space[FIRST3][1][0], space[FIRST3][3][0]
        own, old = get(kept[RATE1]), get(kept[BEFORE1])
        source = get(kept[RATE0])
        zones = [left, own[0], own[1], right]
        k = [16.0 * x for x in stiff()]
        change = curve(zones, mass()[1:4], k[1:3])
        put(kept[BASE_P], [old[i] + 4.0 * source[i + 1] - change[i] for i in (0, 1)])
        put(kept[BASE_X], [left, own[0], own[1]])

    space_wait(LATE)
    zones = zones_of(LATE, get(space[LATE][0]))
    x0, own = get(kept[TOTAL]), get(kept[BEFORE])
    value = [zones[1] - x0[0], own[0], own[1], zones[4] - x0[3]]
    one, sums, two = coarse_pair(zones, value, None)
    put(group[ONCE][0], zones[1:4] + one[1:3])
    group_send(ONCE)
    put(group[TWICE][0], sums[:3] + two)
    group_send(TWICE)

    def velocity(planes, scale, base, out):
        for i, (a, b, c) in enumerate(corner_forces(planes)):
            m = scale * inv_mass[i]
            out[0, 0, i] = base(0, i) + (0.5 * m) * (a + b)
            out[0, 1, i] = base(1, i) + (0.5 * m) * (a - b)
            out[0, 2, i] = base(2, i) + m * c

    stored = [
        pltpu.make_async_copy(near_out[i], far_out[i], out_sems.at[i]) for i in range(4)
    ]
    group_wait(GUESS)
    group_wait(EARLY)
    group_wait(SUMS)
    early, added = get(group[EARLY][1]), get(group[SUMS][1])
    start = get(kept[START])
    velocity(
        [early[i + 2] + 4.0 * added[i] - start[i] for i in range(3)],
        0.5 * FINE,
        lambda c, i: group[GUESS][1][0, c, i] - gv[0, c, i],
        out_rv,
    )
    stored[3].start()
    group_wait(LAST)
    last = get(group[LAST][1])
    for i in range(2):
        out_rp[0, i] = last[i] - kept[RELAXED][i]
    stored[2].start()
    group_wait(ONCE)
    group_wait(TWICE)
    once, twice = get(group[ONCE][1]), get(group[TWICE][1])
    for i in range(2):
        out_cp[0, i] = kept[BASE_P][i] + (last[i] + early[i]) + once[i + 3] + twice[i + 3]
    stored[0].start()
    velocity(
        [kept[BASE_X][i] + added[i] + once[i] + twice[i] for i in range(3)],
        0.5 * COARSE,
        lambda c, i: iv[c, i],
        out_cv,
    )
    stored[1].start()

    for name in SPACE_MESSAGES:
        pl.when(has_right)(lambda name=name: space_copy(name, True).wait_send())
        pl.when(has_left)(lambda name=name: space_copy(name, False).wait_send())
    for name, (_, ahead) in GROUP_MESSAGES.items():
        pl.when(t + ahead < n_t)(lambda name=name: group_copy(name).wait_send())
    for copy in stored:
        copy.wait()


def write_out(*refs):
    held, sems = refs[8:12], refs[12]
    order = (1, 3, 0, 2)
    fetch = [pltpu.make_async_copy(refs[i], held[i], sems.at[0, i]) for i in range(4)]
    store = [pltpu.make_async_copy(held[i], refs[i + 4], sems.at[1, i]) for i in range(4)]
    for i in order:
        fetch[i].start()
    for i in order:
        fetch[i].wait()
        store[i].start()
    for i in order:
        store[i].wait()


def on_device(*args):
    def planes(n):
        return pltpu.VMEM((n, NY, NZ), jnp.float32)

    scratch = []
    for right, left in SPACE_MESSAGES.values():
        scratch += [planes(right), planes(right), planes(left), planes(left)]
    for name, (n, _) in GROUP_MESSAGES.items():
        if name == GUESS:
            scratch += [planes(1), pltpu.VMEM((1, 3, 2, NY, NZ), jnp.float32)]
        else:
            scratch += [planes(n), planes(n)]
    scratch += [planes(n) for n in KEPT.values()]
    scratch += [pltpu.VMEM(x.shape, x.dtype) for x in args]
    field, vector = (1, 2, NY, NZ), (1, 3, 2, NY, NZ)
    scratch += [pltpu.VMEM(x, jnp.float32) for x in (field, vector, field, vector)]
    scratch += [
        pltpu.SemaphoreType.DMA((len(SPACE_MESSAGES), 4)),
        pltpu.SemaphoreType.DMA((len(GROUP_MESSAGES), 2)),
        pltpu.SemaphoreType.DMA((len(args),)),
        pltpu.SemaphoreType.DMA((4,)),
    ]
    shapes = [jax.ShapeDtypeStruct(x, jnp.float32) for x in (field, vector, field, vector)]
    results = pl.pallas_call(
        kernel,
        out_shape=shapes,
        in_specs=[pl.BlockSpec(memory_space=pltpu.HBM)] * 6,
        out_specs=[pl.BlockSpec(memory_space=pltpu.HBM)] * 4,
        scratch_shapes=scratch,
        compiler_params=pltpu.CompilerParams(
            collective_id=0, has_side_effects=True, vmem_limit_bytes=60 << 20
        ),
        cost_estimate=pl.CostEstimate(
            flops=10_000_000, bytes_accessed=2_000_000, transcendentals=0
        ),
    )(*args)
    return pl.pallas_call(
        write_out,
        out_shape=shapes,
        in_specs=[pl.BlockSpec(memory_space=pltpu.HBM)] * 4,
        out_specs=[pl.BlockSpec(memory_space=pltpu.HBM)] * 4,
        scratch_shapes=[pltpu.VMEM(x.shape, x.dtype) for x in shapes]
        + [pltpu.SemaphoreType.DMA((2, 4))],
        compiler_params=pltpu.CompilerParams(vmem_limit_bytes=60 << 20),
        cost_estimate=pl.CostEstimate(flops=0, bytes_accessed=1_000_000, transcendentals=0),
    )(*results)


def solution(mesh):
    placed = (
        P(TM, SPACE, None, None),
        P(TM, None, SPACE, None, None),
        P(SPACE, None, None),
        P(None, SPACE, None, None),
        P(SPACE, None, None),
        P(SPACE, None, None),
    )
    return jax.shard_map(
        on_device,
        mesh=mesh,
        in_specs=placed,
        out_specs=(
            P(TM, SPACE, None, None),
            P(TM, None, SPACE, None, None),
            P(TM, SPACE, None, None),
            P(TM, None, SPACE, None, None),
        ),
        check_vma=False,
    )
```

time: 230 us -> 57.1 us (0.25); the launches traced: 226 us -> 57 us
  waiting for transfers between devices: 147 us -> 0 us
  Pallas kernels: 0 us -> 56.3 us
  starting transfers between devices: 52.7 us -> 0 us
  other arithmetic: 12 us -> 0 us
  local copies, waits for them, and re-layouts: 11.7 us -> 0 us
  between operations: 3.14 us -> 0.64 us
    ppermute x30 -> x0, waiting for transfers between devices: 147 us -> none  [from_behind(): return lax.ppermute(x, axis, pairs)]
    pallas_call x0 -> x2, Pallas kernels: none -> 56.3 us  [the longest x1 54.5 us: on_device(): pl.pallas_call(kernel, out_shape=shapes, in_specs=[pl.BlockSpec(memory_sp...]
    ppermute x30 -> x0, starting transfers between devices: 52.7 us -> none  [from_behind(): return lax.ppermute(x, axis, pairs)]
    slice x270 -> x0, local copies, waits for them, and re-layouts: 9.1 us -> none  [the longest x193 5.54 us: neighbour_sum(): return values + jnp.roll(values, offset, axis=axis)]
    add x97 -> x0, other arithmetic: 6.32 us -> none  [the longest x66 5.4 us: neighbour_sum(): return values + jnp.roll(values, offset, axis=axis)]
    another operation x74 -> x0, other arithmetic: 2.67 us -> none  [node_forces(): return jnp.stack([force_x, force_y, force_z])]
    unnamed x16 -> x0, local copies, waits for them, and re-layouts: 2.38 us -> none
  transfers between devices with their start and end apart: 30 -> 0, of which waited for: 26 -> 0; matrix products, arithmetic and copies ran while one was open for 3% -> 0% of each run, Pallas kernels for 0% -> 0%
where the time goes in v1:
time: 57.1 us; the launch traced here: 57 us
  Pallas kernels  56.3 us (99%)
  between operations  0.64 us (1%)
    pallas_call x1, Pallas kernels, on_device(): pl.pallas_call(kernel, out_shape=shapes, in_specs=[pl.BlockSpec(memory_sp...  54.5 us
    pallas_call x1, Pallas kernels, on_device(): pl.pallas_call(write_out, out_shape=shapes, in_specs=[pl.BlockSpec(memory...  1.81 us

profile of v1, /device:TPU:56, one launch (start us, length us, event | category | flops | bytes accessed | tf_op | source)
XLA Modules:
  0.0 57.0 jit_solution(6403703003096343597)
XLA Ops:
  0.6 54.5 %shard_map.93 = (f32[1,2,64,128]{3,2,1,0:T(8,128)}, f32[1,3,2,64,128]{4,3,2,1,0:T(8,128)}, f32[1,2,64,128]{3,2,1,0:T(8,128)}, f32[1,3,2,64,128]{4,3,2,1,0:T(8,128)}) custom-call(f32[1,2,64,128]{3,2,1,0:T(8,128)} %gp_far.1, f32[1,3,2,64,128]{4,3,2,1,0:T(8,128)} %gv_far.1, f32[2,64,128]{2,1,0:T(8,128)} %ip_far.1, f32[3,2,64,128]{3,2,1,0:T(8,128)} %iv_far.1, ...), custom_call_target="tpu_custom_call" | custom-call | flops 10000000 | bytes 2000000 | tf_op jit(solution)/shard_map/pallas_call | solution.py:513
  55.1 1.8 %shard_map.94 = (f32[1,2,64,128]{3,2,1,0:T(8,128)}, f32[1,3,2,64,128]{4,3,2,1,0:T(8,128)}, f32[1,2,64,128]{3,2,1,0:T(8,128)}, f32[1,3,2,64,128]{4,3,2,1,0:T(8,128)}) custom-call(f32[1,2,64,128]{3,2,1,0:T(8,128)} %get-tuple-element.8.refs_0_, f32[1,3,2,64,128]{4,3,2,1,0:T(8,128)} %get-tuple-element.9.refs_1_, f32[1,2,64,128]{3,2,1,0:T(8,128)} %get-tuple-element.10.refs_2_, ...), custom_call_target="tpu_custom_call" | custom-call | bytes 1000000 | tf_op jit(solution)/shard_map/pallas_call | solution.py:526

commit v2 on v1

--- a/solution.py
+++ b/solution.py
@@ -13,7 +13,7 @@
 MESH = pl.DeviceIdType.MESH
 SPACE, TM = "space", "tm"
 (STATIC, SPREAD, INITIAL, FINE1, FINE2, FINE3, LATE, FIRST1, FIRST2, FIRST3) = range(10)
-(GUESS, EARLY, SUMS, LAST, ONCE, TWICE) = range(6)
+(GUESS, EARLY, SUMS, LAST, OWN, ONCE, TWICE) = range(7)
 (MASS, STIFF, RATE, BEFORE, TOTAL, FUTURE, START, RELAXED, RATE0, RATE1, BEFORE1, TOTAL1, BASE_P, BASE_X) = range(14)
 
 SPACE_MESSAGES = {
@@ -33,7 +33,8 @@
     EARLY: (5, 1),
     SUMS: (3, 1),
     LAST: (2, 1),
-    ONCE: (5, 2),
+    OWN: (2, 2),
+    ONCE: (3, 2),
     TWICE: (5, 3),
 }
 KEPT = {
@@ -108,7 +109,7 @@
 
 
 def kernel(gp_far, gv_far, ip_far, iv_far, k_far, m_far, *rest):
-    far_out, bufs = rest[:4], list(rest[4:])
+    (out_cp, out_cv, out_rp, out_rv), bufs = rest[:4], list(rest[4:])
     space = {}
     for name in SPACE_MESSAGES:
         space[name] = tuple(bufs.pop(0) for _ in range(4))
@@ -118,15 +119,7 @@
     kept = {name: bufs.pop(0) for name in KEPT}
     near = bufs[:6]
     gp, gv, ip, iv, stiffness, inv_mass = near
-    near_out = bufs[6:10]
-    out_cp, out_cv, out_rp, out_rv = near_out
-    space_sems, group_sems, near_sems, out_sems = bufs[10:]
-
-    fetched = {}
-    far = (gp_far, gv_far, ip_far, iv_far, k_far, m_far)
-    for i in (0, 4, 5, 1, 2, 3):
-        fetched[i] = pltpu.make_async_copy(far[i], near[i], near_sems.at[i])
-        fetched[i].start()
+    ready, space_sems, group_sems, near_sems = bufs[6:]
 
     s, t = lax.axis_index(SPACE), lax.axis_index(TM)
     n_s, n_t = lax.axis_size(SPACE), lax.axis_size(TM)
@@ -172,13 +165,19 @@
 
     barrier = pltpu.get_barrier_semaphore()
 
-    def tell(**where):
+    def tell(where):
         pl.semaphore_signal(barrier, inc=1, device_id=where, device_id_type=MESH)
 
-    pl.when(has_right)(lambda: tell(space=s + 1))
-    pl.when(has_left)(lambda: tell(space=s - 1))
-    for back in range(1, 4):
-        pl.when(t >= back)(lambda back=back: tell(tm=t - back))
+    pl.when(has_right)(lambda: tell({SPACE: s + 1}))
+    pl.when(has_left)(lambda: tell({SPACE: s - 1}))
+    for ahead in range(1, 4):
+        pl.when(t + ahead < n_t)(lambda ahead=ahead: tell({TM: t + ahead}))
+
+    fetched = {}
+    far = (gp_far, gv_far, ip_far, iv_far, k_far, m_far)
+    for i in (0, 4, 5, 1, 2, 3):
+        fetched[i] = pltpu.make_async_copy(far[i], near[i], near_sems.at[i])
+        fetched[i].start()
 
     def put(ref, planes):
         for i, x in enumerate(planes):
@@ -201,21 +200,17 @@
             ref = space[name][3]
             put(ref, [nothing] * ref.shape[0])
 
-    for name in (ONCE, TWICE):
+    for name in (OWN, ONCE, TWICE):
 
         @pl.when(t < GROUP_MESSAGES[name][1])
         def _(name=name):
-            put(group[name][1], [nothing] * 5)
+            put(group[name][1], [nothing] * GROUP_MESSAGES[name][0])
 
     for i in (0, 4, 5):
         fetched[i].wait()
     put(space[STATIC][0], [gp[0, 0], gp[0, 1], stiffness[1], inv_mass[1]])
     put(space[STATIC][2], [gp[0, 0], gp[0, 1], stiffness[0], inv_mass[0], inv_mass[1]])
 
-    peers = has_right.astype(jnp.int32) + has_left.astype(jnp.int32) + (n_t - 1 - t)
-    pl.semaphore_wait(barrier, peers)
-
-    space_send(STATIC)
     fetched[1].wait()
     v0 = [gv[0, i, 0] for i in range(3)]
     v1 = [gv[0, i, 1] for i in range(3)]
@@ -223,7 +218,19 @@
     guess_d1 = spread_down(v1)
     put(space[SPREAD][0], [guess_d1])
     put(space[SPREAD][2], [guess_up, guess_d0])
+
+    peers = has_right.astype(jnp.int32) + has_left.astype(jnp.int32) + t
+    pl.semaphore_wait(barrier, peers)
+    space_send(STATIC)
     space_send(SPREAD)
+    for back in range(1, 4):
+
+        @pl.when(t >= back)
+        def _(back=back):
+            pl.semaphore_signal(
+                ready.at[back - 1], inc=1, device_id={TM: t - back}, device_id_type=MESH
+            )
+
     fetched[2].wait()
     fetched[3].wait()
     v0 = [iv[i, 0] for i in range(3)]
@@ -233,7 +240,6 @@
     put(space[INITIAL][0], [ip[0], ip[1], first_d1])
     put(space[INITIAL][2], [ip[0], ip[1], first_up, first_d0])
     space_send(INITIAL)
-    group_send(GUESS)
 
     def mass():
         return get(kept[MASS])
@@ -286,6 +292,9 @@
     put(space[FIRST1][0], p2)
     put(space[FIRST1][2], p2)
     space_send(FIRST1)
+    for ahead in range(1, 4):
+        pl.when(t + ahead < n_t)(lambda ahead=ahead: pl.semaphore_wait(ready.at[ahead - 1], 1))
+    group_send(GUESS)
     put(kept[RATE1], [rate2[0], rate2[0], rate2[1], rate2[1]])
     put(kept[BEFORE1], [p1[0], p1[3]])
     put(kept[TOTAL1], [x + y for x, y in zip(zones[1:5], p1)])
@@ -397,6 +406,8 @@
     group_send(SUMS)
     put(group[LAST][0], p2)
     group_send(LAST)
+    put(group[OWN][0], moved)
+    group_send(OWN)
     put(kept[TOTAL], total)
     put(kept[BEFORE], [p2[0] + ahead[0], p2[1] + ahead[1]])
 
@@ -418,7 +429,7 @@
     x0, own = get(kept[TOTAL]), get(kept[BEFORE])
     value = [zones[1] - x0[0], own[0], own[1], zones[4] - x0[3]]
     one, sums, two = coarse_pair(zones, value, None)
-    put(group[ONCE][0], zones[1:4] + one[1:3])
+    put(group[ONCE][0], [zones[1]] + one[1:3])
     group_send(ONCE)
     put(group[TWICE][0], sums[:3] + two)
     group_send(TWICE)
@@ -430,9 +441,6 @@
             out[0, 1, i] = base(1, i) + (0.5 * m) * (a - b)
             out[0, 2, i] = base(2, i) + m * c
 
-    stored = [
-        pltpu.make_async_copy(near_out[i], far_out[i], out_sems.at[i]) for i in range(4)
-    ]
     group_wait(GUESS)
     group_wait(EARLY)
     group_wait(SUMS)
@@ -444,47 +452,37 @@
         lambda c, i: group[GUESS][1][0, c, i] - gv[0, c, i],
         out_rv,
     )
-    stored[3].start()
     group_wait(LAST)
     last = get(group[LAST][1])
     for i in range(2):
         out_rp[0, i] = last[i] - kept[RELAXED][i]
-    stored[2].start()
+    group_wait(OWN)
     group_wait(ONCE)
     group_wait(TWICE)
     once, twice = get(group[ONCE][1]), get(group[TWICE][1])
+    once = once[:1] + get(group[OWN][1]) + once[1:]
     for i in range(2):
         out_cp[0, i] = kept[BASE_P][i] + (last[i] + early[i]) + once[i + 3] + twice[i + 3]
-    stored[0].start()
     velocity(
         [kept[BASE_X][i] + added[i] + once[i] + twice[i] for i in range(3)],
         0.5 * COARSE,
         lambda c, i: iv[c, i],
         out_cv,
     )
-    stored[1].start()
 
     for name in SPACE_MESSAGES:
         pl.when(has_right)(lambda name=name: space_copy(name, True).wait_send())
         pl.when(has_left)(lambda name=name: space_copy(name, False).wait_send())
     for name, (_, ahead) in GROUP_MESSAGES.items():
         pl.when(t + ahead < n_t)(lambda name=name: group_copy(name).wait_send())
-    for copy in stored:
+
+
+def write_out(*refs):
+    store = [pltpu.make_async_copy(refs[i], refs[i + 4], refs[8].at[i]) for i in range(4)]
+    for copy in store:
+        copy.start()
+    for copy in store:
         copy.wait()
-
-
-def write_out(*refs):
-    held, sems = refs[8:12], refs[12]
-    order = (1, 3, 0, 2)
-    fetch = [pltpu.make_async_copy(refs[i], held[i], sems.at[0, i]) for i in range(4)]
-    store = [pltpu.make_async_copy(held[i], refs[i + 4], sems.at[1, i]) for i in range(4)]
-    for i in order:
-        fetch[i].start()
-    for i in order:
-        fetch[i].wait()
-        store[i].start()
-    for i in order:
-        store[i].wait()
 
 
 def on_device(*args):
@@ -502,35 +500,33 @@
     scratch += [planes(n) for n in KEPT.values()]
     scratch += [pltpu.VMEM(x.shape, x.dtype) for x in args]
     field, vector = (1, 2, NY, NZ), (1, 3, 2, NY, NZ)
-    scratch += [pltpu.VMEM(x, jnp.float32) for x in (field, vector, field, vector)]
     scratch += [
+        pltpu.SemaphoreType.REGULAR((3,)),
         pltpu.SemaphoreType.DMA((len(SPACE_MESSAGES), 4)),
         pltpu.SemaphoreType.DMA((len(GROUP_MESSAGES), 2)),
         pltpu.SemaphoreType.DMA((len(args),)),
-        pltpu.SemaphoreType.DMA((4,)),
     ]
     shapes = [jax.ShapeDtypeStruct(x, jnp.float32) for x in (field, vector, field, vector)]
     results = pl.pallas_call(
         kernel,
-        out_shape=shapes,
+        out_shape=[pltpu.VMEM(x.shape, x.dtype) for x in shapes],
         in_specs=[pl.BlockSpec(memory_space=pltpu.HBM)] * 6,
-        out_specs=[pl.BlockSpec(memory_space=pltpu.HBM)] * 4,
+        out_specs=[pl.BlockSpec(memory_space=pltpu.VMEM)] * 4,
         scratch_shapes=scratch,
         compiler_params=pltpu.CompilerParams(
-            collective_id=0, has_side_effects=True, vmem_limit_bytes=60 << 20
+            collective_id=0, has_side_effects=True, vmem_limit_bytes=24 << 20
         ),
         cost_estimate=pl.CostEstimate(
             flops=10_000_000, bytes_accessed=2_000_000, transcendentals=0
         ),
-    )(*args)
+    )(*[pltpu.with_memory_space_constraint(x, pltpu.HBM) for x in args])
     return pl.pallas_call(
         write_out,
         out_shape=shapes,
-        in_specs=[pl.BlockSpec(memory_space=pltpu.HBM)] * 4,
+        in_specs=[pl.BlockSpec(memory_space=pltpu.VMEM)] * 4,
         out_specs=[pl.BlockSpec(memory_space=pltpu.HBM)] * 4,
-        scratch_shapes=[pltpu.VMEM(x.shape, x.dtype) for x in shapes]
-        + [pltpu.SemaphoreType.DMA((2, 4))],
-        compiler_params=pltpu.CompilerParams(vmem_limit_bytes=60 << 20),
+        scratch_shapes=[pltpu.SemaphoreType.DMA((4,))],
+        compiler_params=pltpu.CompilerParams(vmem_limit_bytes=24 << 20),
         cost_estimate=pl.CostEstimate(flops=0, bytes_accessed=1_000_000, transcendentals=0),
     )(*results)
 

time: 57.1 us -> 52.3 us (0.916)
  Pallas kernels: 56.3 us -> 51.5 us
    pallas_call x1, Pallas kernels: 54.5 us -> 50.7 us  [on_device(): pl.pallas_call(kernel, out_shape=[pltpu.VMEM(x.shape, x.dtype) for x in s...]
    pallas_call x1, Pallas kernels: 1.81 us -> 0.82 us  [on_device(): pl.pallas_call(write_out, out_shape=shapes, in_specs=[pl.BlockSpec(memory...]
where the time goes in v2:
time: 52.3 us; the launch traced here: 52.2 us
  Pallas kernels  51.5 us (98%)
  between operations  0.64 us (1%)
    pallas_call x1, Pallas kernels, on_device(): pl.pallas_call(kernel, out_shape=[pltpu.VMEM(x.shape, x.dtype) for x in s...  50.7 us

profile of v2, /device:TPU:56, one launch (start us, length us, event | category | flops | bytes accessed | tf_op | source)
XLA Modules:
  0.0 52.2 jit_solution(17222643836813331991)
XLA Ops:
  0.6 50.7 %shard_map.93 = (f32[1,2,64,128]{3,2,1,0:T(8,128)S(1)}, f32[1,3,2,64,128]{4,3,2,1,0:T(8,128)S(1)}, f32[1,2,64,128]{3,2,1,0:T(8,128)S(1)}, f32[1,3,2,64,128]{4,3,2,1,0:T(8,128)S(1)}) custom-call(f32[1,2,64,128]{3,2,1,0:T(8,128)} %gp_far.1, f32[1,3,2,64,128]{4,3,2,1,0:T(8,128)} %gv_far.1, f32[2,64,128]{2,1,0:T(8,128)} %ip_far.1, f32[3,2,64,128]{3,2,1,0:T(8,128)} %iv_far.1, ...), custom_call_target="tpu_custom_call" | custom-call | flops 10000000 | bytes 2000000 | tf_op jit(solution)/shard_map/pallas_call | solution.py:510
  51.4 0.8 %shard_map.94 = (f32[1,2,64,128]{3,2,1,0:T(8,128)}, f32[1,3,2,64,128]{4,3,2,1,0:T(8,128)}, f32[1,2,64,128]{3,2,1,0:T(8,128)}, f32[1,3,2,64,128]{4,3,2,1,0:T(8,128)}) custom-call(f32[1,2,64,128]{3,2,1,0:T(8,128)S(1)} %get-tuple-element.8.refs_0_, f32[1,3,2,64,128]{4,3,2,1,0:T(8,128)S(1)} %get-tuple-element.9.refs_1_, ...), custom_call_target="tpu_custom_call" | custom-call | bytes 1000000 | tf_op jit(solution)/shard_map/pallas_call | solution.py:523

commit v3 on v2

--- a/solution.py
+++ b/solution.py
@@ -13,7 +13,7 @@
 MESH = pl.DeviceIdType.MESH
 SPACE, TM = "space", "tm"
 (STATIC, SPREAD, INITIAL, FINE1, FINE2, FINE3, LATE, FIRST1, FIRST2, FIRST3) = range(10)
-(GUESS, EARLY, SUMS, LAST, OWN, ONCE, TWICE) = range(7)
+(GUESS, MID, EARLY, SUMS, LAST, RELAY, ONCE, TWICE, THEN) = range(9)
 (MASS, STIFF, RATE, BEFORE, TOTAL, FUTURE, START, RELAXED, RATE0, RATE1, BEFORE1, TOTAL1, BASE_P, BASE_X) = range(14)
 
 SPACE_MESSAGES = {
@@ -29,13 +29,15 @@
     FIRST3: (1, 1),
 }
 GROUP_MESSAGES = {
-    GUESS: (6, 1),
-    EARLY: (5, 1),
-    SUMS: (3, 1),
-    LAST: (2, 1),
-    OWN: (2, 2),
-    ONCE: (3, 2),
-    TWICE: (5, 3),
+    GUESS: (6, 1, 0),
+    MID: (2, 1, 0),
+    EARLY: (3, 1, 0),
+    SUMS: (3, 1, 0),
+    LAST: (2, 1, 0),
+    RELAY: (2, 1, 1),
+    ONCE: (3, 2, 0),
+    TWICE: (3, 3, 0),
+    THEN: (2, 3, 0),
 }
 KEPT = {
     MASS: 5,
@@ -157,11 +159,22 @@
             device_id_type=MESH,
         )
 
+    def sends_on(name):
+        _, ahead, first = GROUP_MESSAGES[name]
+        return (t >= first) & (t + ahead < n_t)
+
+    def hears(name):
+        _, ahead, first = GROUP_MESSAGES[name]
+        return t >= ahead + first
+
+    def heard(ahead):
+        pl.when(t + ahead < n_t)(lambda: pl.semaphore_wait(ready.at[ahead - 1], 1))
+
     def group_send(name):
-        pl.when(t + GROUP_MESSAGES[name][1] < n_t)(lambda: group_copy(name).start())
+        pl.when(sends_on(name))(lambda: group_copy(name).start())
 
     def group_wait(name):
-        pl.when(t >= GROUP_MESSAGES[name][1])(lambda: group_copy(name).wait_recv())
+        pl.when(hears(name))(lambda: group_copy(name).wait_recv())
 
     barrier = pltpu.get_barrier_semaphore()
 
@@ -200,9 +213,9 @@
             ref = space[name][3]
             put(ref, [nothing] * ref.shape[0])
 
-    for name in (OWN, ONCE, TWICE):
-
-        @pl.when(t < GROUP_MESSAGES[name][1])
+    for name in (RELAY, ONCE, TWICE, THEN):
+
+        @pl.when(jnp.logical_not(hears(name)))
         def _(name=name):
             put(group[name][1], [nothing] * GROUP_MESSAGES[name][0])
 
@@ -277,6 +290,8 @@
     put(space[FINE1][0], p2)
     put(space[FINE1][2], p2)
     space_send(FINE1)
+    heard(1)
+    group_send(GUESS)
     put(kept[RATE], [rate2[0], rate2[0], rate2[1], rate2[1]])
     put(kept[BEFORE], [p1[0], p1[3]])
     put(kept[TOTAL], [x + y for x, y in zip(zones[1:5], p1)])
@@ -292,9 +307,6 @@
     put(space[FIRST1][0], p2)
     put(space[FIRST1][2], p2)
     space_send(FIRST1)
-    for ahead in range(1, 4):
-        pl.when(t + ahead < n_t)(lambda ahead=ahead: pl.semaphore_wait(ready.at[ahead - 1], 1))
-    group_send(GUESS)
     put(kept[RATE1], [rate2[0], rate2[0], rate2[1], rate2[1]])
     put(kept[BEFORE1], [p1[0], p1[3]])
     put(kept[TOTAL1], [x + y for x, y in zip(zones[1:5], p1)])
@@ -313,6 +325,8 @@
     put(kept[TOTAL], total)
     put(kept[START], total[:3])
     put(kept[RELAXED], p2)
+    put(group[MID][0], [total[1] + 4.0 * p2[0], total[2] + 4.0 * p2[1]])
+    group_send(MID)
 
     space_wait(FIRST1)
     zones = zones_of(FIRST1, get(space[FIRST1][0]))
@@ -330,7 +344,8 @@
     def _():
         put(kept[BASE_P], p2)
         put(kept[BASE_X], [0.25 * x for x in total1[:3]])
-        put(group[EARLY][1], [-p2[0], -p2[1]] + total1[:3])
+        put(group[EARLY][1], [-p2[0], -p2[1], total1[0]])
+        put(group[MID][1], total1[1:3])
         put(group[SUMS][1], [nothing] * 3)
         put(group[LAST][1], p2)
         for i in range(3):
@@ -348,31 +363,34 @@
     put(space[FINE3][2], p2)
     space_send(FINE3)
     ahead = [12.0 * rate[i] - 16.0 * rate1[i] - zones[i + 1] for i in (1, 2)]
-    sums = [x + 4.0 * y for x, y in zip(get(kept[START]), zones[1:4])]
-    put(group[EARLY][0], ahead + sums)
+    put(group[EARLY][0], ahead + [kept[START][0] + 4.0 * zones[1]])
     group_send(EARLY)
     put(kept[FUTURE], ahead + ahead)
     put(kept[RATE], [rate2[0], rate2[0], rate2[1], rate2[1]])
     put(kept[BEFORE], [p1[0], p1[3]])
     put(kept[TOTAL], [0.25 * (y - 3.0 * x) for x, y in zip(zones[1:5], p1)])
 
-    def coarse_pair(zones, value, source):
-        m, k = mass(), [16.0 * x for x in stiff()]
-        one = [x - c for x, c in zip(value, curve(zones, m, k))]
+    def coarse_first(zones, value, source):
+        k = [16.0 * x for x in stiff()]
+        one = [x - c for x, c in zip(value, curve(zones, mass(), k))]
         if source is not None:
             one = [x + y for x, y in zip(one, source)]
-        sums = [x + y for x, y in zip(zones[1:5], one)]
-        two = [x - c for x, c in zip(one[1:3], curve(sums, m[1:4], k[1:3]))]
+        return one, [x + y for x, y in zip(zones[1:5], one)]
+
+    def coarse_second(one, sums, source):
+        k = [16.0 * x for x in stiff()]
+        two = [x - c for x, c in zip(one[1:3], curve(sums, mass()[1:4], k[1:3]))]
         if source is not None:
             two = [x + y for x, y in zip(two, source[1:3])]
-        return one, sums, two
+        return two
 
     space_wait(FIRST2)
     zones = zones_of(FIRST2, get(space[FIRST2][0]))
     x0, own = get(kept[TOTAL1]), get(kept[BEFORE1])
     value = [zones[1] - x0[0], own[0], own[1], zones[4] - x0[3]]
     source = [4.0 * x for x in get(kept[RATE0])]
-    one, sums, two = coarse_pair(zones, value, source)
+    one, sums = coarse_first(zones, value, source)
+    two = coarse_second(one, sums, source)
     third = [sums[1] + two[0], sums[2] + two[1]]
     put(space[FIRST3][0], [third[1]])
     put(space[FIRST3][2], [third[0]])
@@ -406,8 +424,6 @@
     group_send(SUMS)
     put(group[LAST][0], p2)
     group_send(LAST)
-    put(group[OWN][0], moved)
-    group_send(OWN)
     put(kept[TOTAL], total)
     put(kept[BEFORE], [p2[0] + ahead[0], p2[1] + ahead[1]])
 
@@ -428,11 +444,22 @@
     zones = zones_of(LATE, get(space[LATE][0]))
     x0, own = get(kept[TOTAL]), get(kept[BEFORE])
     value = [zones[1] - x0[0], own[0], own[1], zones[4] - x0[3]]
-    one, sums, two = coarse_pair(zones, value, None)
+    one, sums = coarse_first(zones, value, None)
+    put(group[TWICE][0], sums[:3])
+    heard(3)
+    group_send(TWICE)
     put(group[ONCE][0], [zones[1]] + one[1:3])
+    heard(2)
     group_send(ONCE)
-    put(group[TWICE][0], sums[:3] + two)
-    group_send(TWICE)
+    put(group[THEN][0], coarse_second(one, sums, None))
+    group_send(THEN)
+
+    group_wait(EARLY)
+    group_wait(SUMS)
+    group_wait(LAST)
+    early, added, last = get(group[EARLY][1]), get(group[SUMS][1]), get(group[LAST][1])
+    put(group[RELAY][0], [added[i + 1] + (last[i] + early[i]) for i in (0, 1)])
+    group_send(RELAY)
 
     def velocity(planes, scale, base, out):
         for i, (a, b, c) in enumerate(corner_forces(planes)):
@@ -442,25 +469,24 @@
             out[0, 2, i] = base(2, i) + m * c
 
     group_wait(GUESS)
-    group_wait(EARLY)
-    group_wait(SUMS)
-    early, added = get(group[EARLY][1]), get(group[SUMS][1])
+    group_wait(MID)
+    early, added, last = get(group[EARLY][1]), get(group[SUMS][1]), get(group[LAST][1])
+    whole = early[2:] + get(group[MID][1])
     start = get(kept[START])
     velocity(
-        [early[i + 2] + 4.0 * added[i] - start[i] for i in range(3)],
+        [whole[i] + 4.0 * added[i] - start[i] for i in range(3)],
         0.5 * FINE,
         lambda c, i: group[GUESS][1][0, c, i] - gv[0, c, i],
         out_rv,
     )
-    group_wait(LAST)
-    last = get(group[LAST][1])
     for i in range(2):
         out_rp[0, i] = last[i] - kept[RELAXED][i]
-    group_wait(OWN)
+    group_wait(RELAY)
     group_wait(ONCE)
     group_wait(TWICE)
-    once, twice = get(group[ONCE][1]), get(group[TWICE][1])
-    once = once[:1] + get(group[OWN][1]) + once[1:]
+    group_wait(THEN)
+    once, twice = get(group[ONCE][1]), get(group[TWICE][1]) + get(group[THEN][1])
+    once = once[:1] + get(group[RELAY][1]) + once[1:]
     for i in range(2):
         out_cp[0, i] = kept[BASE_P][i] + (last[i] + early[i]) + once[i + 3] + twice[i + 3]
     velocity(
@@ -473,8 +499,8 @@
     for name in SPACE_MESSAGES:
         pl.when(has_right)(lambda name=name: space_copy(name, True).wait_send())
         pl.when(has_left)(lambda name=name: space_copy(name, False).wait_send())
-    for name, (_, ahead) in GROUP_MESSAGES.items():
-        pl.when(t + ahead < n_t)(lambda name=name: group_copy(name).wait_send())
+    for name in GROUP_MESSAGES:
+        pl.when(sends_on(name))(lambda name=name: group_copy(name).wait_send())
 
 
 def write_out(*refs):
@@ -492,7 +518,7 @@
     scratch = []
     for right, left in SPACE_MESSAGES.values():
         scratch += [planes(right), planes(right), planes(left), planes(left)]
-    for name, (n, _) in GROUP_MESSAGES.items():
+    for name, (n, _, _) in GROUP_MESSAGES.items():
         if name == GUESS:
             scratch += [planes(1), pltpu.VMEM((1, 3, 2, NY, NZ), jnp.float32)]
         else:

time: 52.3 us -> 51.9 us (level)
  no operation moved by 1% of the time
where the time goes in v3:
time: 51.9 us; the launch traced here: 51.8 us
  Pallas kernels  51.1 us (98%)
  between operations  0.64 us (1%)
    pallas_call x1, Pallas kernels, on_device(): pl.pallas_call(kernel, out_shape=[pltpu.VMEM(x.shape, x.dtype) for x in s...  50.3 us

profile of v3, /device:TPU:56, one launch (start us, length us, event | category | flops | bytes accessed | tf_op | source)
XLA Modules:
  0.0 51.8 jit_solution(4443242645382364352)
XLA Ops:
  0.6 50.3 %shard_map.93 = (f32[1,2,64,128]{3,2,1,0:T(8,128)S(1)}, f32[1,3,2,64,128]{4,3,2,1,0:T(8,128)S(1)}, f32[1,2,64,128]{3,2,1,0:T(8,128)S(1)}, f32[1,3,2,64,128]{4,3,2,1,0:T(8,128)S(1)}) custom-call(f32[1,2,64,128]{3,2,1,0:T(8,128)} %gp_far.1, f32[1,3,2,64,128]{4,3,2,1,0:T(8,128)} %gv_far.1, f32[2,64,128]{2,1,0:T(8,128)} %ip_far.1, f32[3,2,64,128]{3,2,1,0:T(8,128)} %iv_far.1, ...), custom_call_target="tpu_custom_call" | custom-call | flops 10000000 | bytes 2000000 | tf_op jit(solution)/shard_map/pallas_call | solution.py:536
  50.9 0.8 %shard_map.94 = (f32[1,2,64,128]{3,2,1,0:T(8,128)}, f32[1,3,2,64,128]{4,3,2,1,0:T(8,128)}, f32[1,2,64,128]{3,2,1,0:T(8,128)}, f32[1,3,2,64,128]{4,3,2,1,0:T(8,128)}) custom-call(f32[1,2,64,128]{3,2,1,0:T(8,128)S(1)} %get-tuple-element.8.refs_0_, f32[1,3,2,64,128]{4,3,2,1,0:T(8,128)S(1)} %get-tuple-element.9.refs_1_, ...), custom_call_target="tpu_custom_call" | custom-call | bytes 1000000 | tf_op jit(solution)/shard_map/pallas_call | solution.py:549

commit v4 on v3

--- a/solution.py
+++ b/solution.py
@@ -28,6 +28,7 @@
     FIRST2: (2, 2),
     FIRST3: (1, 1),
 }
+ONWARD = (FINE2, FINE3, LATE)
 GROUP_MESSAGES = {
     GUESS: (6, 1, 0),
     MID: (2, 1, 0),
@@ -73,13 +74,15 @@
     return pltpu.roll(x, NZ - 1, 1)
 
 
+def zone_part(x):
+    below = lower_z(x)
+    s = below + x
+    t = 0.5 * (below - x)
+    return s, lower_y(s), t + lower_y(t)
+
+
 def corner_forces(zones):
-    parts = []
-    for x in zones:
-        below = lower_z(x)
-        s = below + x
-        t = 0.5 * (below - x)
-        parts.append((s, lower_y(s), t + lower_y(t)))
+    parts = [x if isinstance(x, tuple) else zone_part(x) for x in zones]
     forces = []
     for (s0, r0, t0), (s1, r1, t1) in zip(parts[:-1], parts[1:]):
         forces.append((r0 - s1, s0 - r1, t0 + t1))
@@ -126,12 +129,19 @@
     s, t = lax.axis_index(SPACE), lax.axis_index(TM)
     n_s, n_t = lax.axis_size(SPACE), lax.axis_size(TM)
     has_left, has_right = s > 0, s < n_s - 1
+    goes_on = t + 1 < n_t
+
+    def to_right(name):
+        return has_right & goes_on if name in ONWARD else has_right
+
+    def to_left(name):
+        return has_left & goes_on if name in ONWARD else has_left
 
     def space_copy(name, right):
         i = name
-        to_right, from_left, to_left, from_right = space[name]
+        out_right, from_left, out_left, from_right = space[name]
         return pltpu.make_async_remote_copy(
-            src_ref=to_right if right else to_left,
+            src_ref=out_right if right else out_left,
             dst_ref=from_left if right else from_right,
             send_sem=space_sems.at[i, 0 if right else 1],
             recv_sem=space_sems.at[i, 2 if right else 3],
@@ -140,12 +150,14 @@
         )
 
     def space_send(name):
-        pl.when(has_right)(lambda: space_copy(name, True).start())
-        pl.when(has_left)(lambda: space_copy(name, False).start())
+        odd = lax.rem(s, 2) == 1
+        pl.when(to_right(name) & odd)(lambda: space_copy(name, True).start())
+        pl.when(to_left(name))(lambda: space_copy(name, False).start())
+        pl.when(to_right(name) & jnp.logical_not(odd))(lambda: space_copy(name, True).start())
 
     def space_wait(name):
-        pl.when(has_left)(lambda: space_copy(name, True).wait_recv())
-        pl.when(has_right)(lambda: space_copy(name, False).wait_recv())
+        pl.when(to_left(name))(lambda: space_copy(name, True).wait_recv())
+        pl.when(to_right(name))(lambda: space_copy(name, False).wait_recv())
 
     def group_copy(name):
         i = name
@@ -213,6 +225,12 @@
             ref = space[name][3]
             put(ref, [nothing] * ref.shape[0])
 
+    @pl.when(jnp.logical_not(goes_on))
+    def _():
+        for name in ONWARD:
+            put(space[name][1], [nothing] * 2)
+            put(space[name][3], [nothing] * 2)
+
     for name in (RELAY, ONCE, TWICE, THEN):
 
         @pl.when(jnp.logical_not(hears(name)))
@@ -260,9 +278,10 @@
     def stiff(scale=None):
         return get(kept[STIFF])
 
-    def fine_pair(zones, rate):
+    def fine_pair(zones, rate, own=None):
         m, k = mass(), stiff()
-        rate = [r - c for r, c in zip(rate, curve(zones, m, k))]
+        parts = zones[:2] + (own or zones[2:4]) + zones[4:]
+        rate = [r - c for r, c in zip(rate, curve(parts, m, k))]
         p1 = [x + r for x, r in zip(zones[1:-1], rate)]
         rate2 = [r - c for r, c in zip(rate[1:3], curve(p1, m[1:4], k[1:3]))]
         p2 = [x + r for x, r in zip(p1[1:3], rate2)]
@@ -275,6 +294,7 @@
     def next_rate(zones, before, own):
         return [zones[1] - before[0], own[0], own[1], zones[4] - before[1]]
 
+    own_parts = [zone_part(gp[0, 0]), zone_part(gp[0, 1])]
     space_wait(STATIC)
     left, right = get(space[STATIC][1]), get(space[STATIC][3])
     put(kept[MASS], [left[3], inv_mass[0], inv_mass[1], right[3], right[4]])
@@ -286,7 +306,7 @@
     left, right = get(space[SPREAD][1]), get(space[SPREAD][3])
     spread = [left[0] + guess_up, guess_d0, guess_d1 + right[0], right[1]]
     rate = [(-0.25 * FINE) * k * d for k, d in zip(raw, spread)]
-    p1, rate1, p2, rate2 = fine_pair(zones, rate)
+    p1, rate1, p2, rate2 = fine_pair(zones, rate, own_parts)
     put(space[FINE1][0], p2)
     put(space[FINE1][2], p2)
     space_send(FINE1)
@@ -311,11 +331,12 @@
     put(kept[BEFORE1], [p1[0], p1[3]])
     put(kept[TOTAL1], [x + y for x, y in zip(zones[1:5], p1)])
 
+    own_parts = [zone_part(x) for x in get(space[FINE1][0])]
     space_wait(FINE1)
     zones = zones_of(FINE1, get(space[FINE1][0]))
     old = get(kept[RATE])
     rate = next_rate(zones, get(kept[BEFORE]), [old[1], old[2]])
-    p1, rate1, p2, rate2 = fine_pair(zones, rate)
+    p1, rate1, p2, rate2 = fine_pair(zones, rate, own_parts)
     put(space[FINE2][0], p2)
     put(space[FINE2][2], p2)
     space_send(FINE2)
@@ -354,11 +375,12 @@
 
     put(kept[BEFORE1], p2)
 
+    own_parts = [zone_part(x) for x in get(space[FINE2][0])]
     space_wait(FINE2)
     zones = zones_of(FINE2, get(space[FINE2][0]))
     old = get(kept[RATE])
     rate = next_rate(zones, get(kept[BEFORE]), [old[1], old[2]])
-    p1, rate1, p2, rate2 = fine_pair(zones, rate)
+    p1, rate1, p2, rate2 = fine_pair(zones, rate, own_parts)
     put(space[FINE3][0], p2)
     put(space[FINE3][2], p2)
     space_send(FINE3)
@@ -370,9 +392,10 @@
     put(kept[BEFORE], [p1[0], p1[3]])
     put(kept[TOTAL], [0.25 * (y - 3.0 * x) for x, y in zip(zones[1:5], p1)])
 
-    def coarse_first(zones, value, source):
+    def coarse_first(zones, value, source, own=None):
         k = [16.0 * x for x in stiff()]
-        one = [x - c for x, c in zip(value, curve(zones, mass(), k))]
+        parts = zones[:2] + (own or zones[2:4]) + zones[4:]
+        one = [x - c for x, c in zip(value, curve(parts, mass(), k))]
         if source is not None:
             one = [x + y for x, y in zip(one, source)]
         return one, [x + y for x, y in zip(zones[1:5], one)]
@@ -384,36 +407,12 @@
             two = [x + y for x, y in zip(two, source[1:3])]
         return two
 
-    space_wait(FIRST2)
-    zones = zones_of(FIRST2, get(space[FIRST2][0]))
-    x0, own = get(kept[TOTAL1]), get(kept[BEFORE1])
-    value = [zones[1] - x0[0], own[0], own[1], zones[4] - x0[3]]
-    source = [4.0 * x for x in get(kept[RATE0])]
-    one, sums = coarse_first(zones, value, source)
-    two = coarse_second(one, sums, source)
-    third = [sums[1] + two[0], sums[2] + two[1]]
-    put(space[FIRST3][0], [third[1]])
-    put(space[FIRST3][2], [third[0]])
-    space_send(FIRST3)
-
-    @pl.when(t == 1)
-    def _():
-        put(kept[BASE_P], one[1:3])
-        put(kept[BASE_X], zones[1:4])
-
-    @pl.when(t == 2)
-    def _():
-        put(kept[BASE_P], two)
-        put(kept[BASE_X], sums[:3])
-
-    put(kept[BEFORE1], two)
-    put(kept[RATE1], third + third)
-
+    own_parts = [zone_part(x) for x in get(space[FINE3][0])]
     space_wait(FINE3)
     zones = zones_of(FINE3, get(space[FINE3][0]))
     old = get(kept[RATE])
     rate = next_rate(zones, get(kept[BEFORE]), [old[1], old[2]])
-    p1, rate1, p2, rate2 = fine_pair(zones, rate)
+    p1, rate1, p2, rate2 = fine_pair(zones, rate, own_parts)
     total = [x + 0.25 * (y + z) for x, y, z in zip(get(kept[TOTAL]), zones[1:5], p1)]
     ahead = get(kept[FUTURE])
     moved = [total[i + 1] + p2[i] + ahead[i] for i in (0, 1)]
@@ -427,6 +426,53 @@
     put(kept[TOTAL], total)
     put(kept[BEFORE], [p2[0] + ahead[0], p2[1] + ahead[1]])
 
+    space_wait(FIRST2)
+    zones = zones_of(FIRST2, get(space[FIRST2][0]))
+    x0, own = get(kept[TOTAL1]), get(kept[BEFORE1])
+    value = [zones[1] - x0[0], own[0], own[1], zones[4] - x0[3]]
+    source = [4.0 * x for x in get(kept[RATE0])]
+    one, sums = coarse_first(zones, value, source)
+    two = coarse_second(one, sums, source)
+    third = [sums[1] + two[0], sums[2] + two[1]]
+    put(space[FIRST3][0], [third[1]])
+    put(space[FIRST3][2], [third[0]])
+    space_send(FIRST3)
+
+    @pl.when(t == 1)
+    def _():
+        put(kept[BASE_P], one[1:3])
+        put(kept[BASE_X], zones[1:4])
+
+    @pl.when(t == 2)
+    def _():
+        put(kept[BASE_P], two)
+        put(kept[BASE_X], sums[:3])
+
+    put(kept[BEFORE1], two)
+    put(kept[RATE1], third + third)
+
+    own_parts = [zone_part(x) for x in get(space[LATE][0])]
+    space_wait(LATE)
+    zones = zones_of(LATE, get(space[LATE][0]))
+    x0, own = get(kept[TOTAL]), get(kept[BEFORE])
+    value = [zones[1] - x0[0], own[0], own[1], zones[4] - x0[3]]
+    one, sums = coarse_first(zones, value, None, own_parts)
+    put(group[TWICE][0], sums[:3])
+    heard(3)
+    group_send(TWICE)
+    put(group[ONCE][0], [zones[1]] + one[1:3])
+    heard(2)
+    group_send(ONCE)
+    put(group[THEN][0], coarse_second(one, sums, None))
+    group_send(THEN)
+
+    group_wait(EARLY)
+    group_wait(SUMS)
+    group_wait(LAST)
+    early, added, last = get(group[EARLY][1]), get(group[SUMS][1]), get(group[LAST][1])
+    put(group[RELAY][0], [added[i + 1] + (last[i] + early[i]) for i in (0, 1)])
+    group_send(RELAY)
+
     space_wait(FIRST3)
 
     @pl.when(t == 3)
@@ -439,27 +485,6 @@
         change = curve(zones, mass()[1:4], k[1:3])
         put(kept[BASE_P], [old[i] + 4.0 * source[i + 1] - change[i] for i in (0, 1)])
         put(kept[BASE_X], [left, own[0], own[1]])
-
-    space_wait(LATE)
-    zones = zones_of(LATE, get(space[LATE][0]))
-    x0, own = get(kept[TOTAL]), get(kept[BEFORE])
-    value = [zones[1] - x0[0], own[0], own[1], zones[4] - x0[3]]
-    one, sums = coarse_first(zones, value, None)
-    put(group[TWICE][0], sums[:3])
-    heard(3)
-    group_send(TWICE)
-    put(group[ONCE][0], [zones[1]] + one[1:3])
-    heard(2)
-    group_send(ONCE)
-    put(group[THEN][0], coarse_second(one, sums, None))
-    group_send(THEN)
-
-    group_wait(EARLY)
-    group_wait(SUMS)
-    group_wait(LAST)
-    early, added, last = get(group[EARLY][1]), get(group[SUMS][1]), get(group[LAST][1])
-    put(group[RELAY][0], [added[i + 1] + (last[i] + early[i]) for i in (0, 1)])
-    group_send(RELAY)
 
     def velocity(planes, scale, base, out):
         for i, (a, b, c) in enumerate(corner_forces(planes)):
@@ -497,8 +522,8 @@
     )
 
     for name in SPACE_MESSAGES:
-        pl.when(has_right)(lambda name=name: space_copy(name, True).wait_send())
-        pl.when(has_left)(lambda name=name: space_copy(name, False).wait_send())
+        pl.when(to_right(name))(lambda name=name: space_copy(name, True).wait_send())
+        pl.when(to_left(name))(lambda name=name: space_copy(name, False).wait_send())
     for name in GROUP_MESSAGES:
         pl.when(sends_on(name))(lambda name=name: group_copy(name).wait_send())
 

time: 51.9 us -> 51.8 us (level)
  no operation moved by 1% of the time
where the time goes in v4:
time: 51.8 us; the launch traced here: 51.6 us
  Pallas kernels  51 us (98%)
  between operations  0.64 us (1%)
    pallas_call x1, Pallas kernels, on_device(): pl.pallas_call(kernel, out_shape=[pltpu.VMEM(x.shape, x.dtype) for x in s...  50.1 us

profile of v4, /device:TPU:56, one launch (start us, length us, event | category | flops | bytes accessed | tf_op | source)
XLA Modules:
  0.0 51.6 jit_solution(2796521675023736296)
XLA Ops:
  0.6 50.1 %shard_map.93 = (f32[1,2,64,128]{3,2,1,0:T(8,128)S(1)}, f32[1,3,2,64,128]{4,3,2,1,0:T(8,128)S(1)}, f32[1,2,64,128]{3,2,1,0:T(8,128)S(1)}, f32[1,3,2,64,128]{4,3,2,1,0:T(8,128)S(1)}) custom-call(f32[1,2,64,128]{3,2,1,0:T(8,128)} %gp_far.1, f32[1,3,2,64,128]{4,3,2,1,0:T(8,128)} %gv_far.1, f32[2,64,128]{2,1,0:T(8,128)} %ip_far.1, f32[3,2,64,128]{3,2,1,0:T(8,128)} %iv_far.1, ...), custom_call_target="tpu_custom_call" | custom-call | flops 10000000 | bytes 2000000 | tf_op jit(solution)/shard_map/pallas_call | solution.py:561
  50.8 0.8 %shard_map.94 = (f32[1,2,64,128]{3,2,1,0:T(8,128)}, f32[1,3,2,64,128]{4,3,2,1,0:T(8,128)}, f32[1,2,64,128]{3,2,1,0:T(8,128)}, f32[1,3,2,64,128]{4,3,2,1,0:T(8,128)}) custom-call(f32[1,2,64,128]{3,2,1,0:T(8,128)S(1)} %get-tuple-element.8.refs_0_, f32[1,3,2,64,128]{4,3,2,1,0:T(8,128)S(1)} %get-tuple-element.9.refs_1_, ...), custom_call_target="tpu_custom_call" | custom-call | bytes 1000000 | tf_op jit(solution)/shard_map/pallas_call | solution.py:574

commit v5 on v4

--- a/solution.py
+++ b/solution.py
@@ -303,6 +303,8 @@
     put(kept[STIFF], [scale * k for k in raw])
     zones = left[:2] + [gp[0, 0], gp[0, 1]] + right[:2]
     space_wait(SPREAD)
+    heard(1)
+    group_send(GUESS)
     left, right = get(space[SPREAD][1]), get(space[SPREAD][3])
     spread = [left[0] + guess_up, guess_d0, guess_d1 + right[0], right[1]]
     rate = [(-0.25 * FINE) * k * d for k, d in zip(raw, spread)]
@@ -310,8 +312,6 @@
     put(space[FINE1][0], p2)
     put(space[FINE1][2], p2)
     space_send(FINE1)
-    heard(1)
-    group_send(GUESS)
     put(kept[RATE], [rate2[0], rate2[0], rate2[1], rate2[1]])
     put(kept[BEFORE], [p1[0], p1[3]])
     put(kept[TOTAL], [x + y for x, y in zip(zones[1:5], p1)])

time: 51.8 us -> 51.8 us (level)
  no operation moved by 1% of the time
where the time goes in v5:
time: 51.8 us; the launch traced here: 51.6 us
  Pallas kernels  51 us (98%)
  between operations  0.64 us (1%)
    pallas_call x1, Pallas kernels, on_device(): pl.pallas_call(kernel, out_shape=[pltpu.VMEM(x.shape, x.dtype) for x in s...  50.1 us

profile of v5, /device:TPU:56, one launch (start us, length us, event | category | flops | bytes accessed | tf_op | source)
XLA Modules:
  0.0 51.6 jit_solution(194575459269897326)
XLA Ops:
  0.6 50.1 %shard_map.93 = (f32[1,2,64,128]{3,2,1,0:T(8,128)S(1)}, f32[1,3,2,64,128]{4,3,2,1,0:T(8,128)S(1)}, f32[1,2,64,128]{3,2,1,0:T(8,128)S(1)}, f32[1,3,2,64,128]{4,3,2,1,0:T(8,128)S(1)}) custom-call(f32[1,2,64,128]{3,2,1,0:T(8,128)} %gp_far.1, f32[1,3,2,64,128]{4,3,2,1,0:T(8,128)} %gv_far.1, f32[2,64,128]{2,1,0:T(8,128)} %ip_far.1, f32[3,2,64,128]{3,2,1,0:T(8,128)} %iv_far.1, ...), custom_call_target="tpu_custom_call" | custom-call | flops 10000000 | bytes 2000000 | tf_op jit(solution)/shard_map/pallas_call | solution.py:561
  50.8 0.8 %shard_map.94 = (f32[1,2,64,128]{3,2,1,0:T(8,128)}, f32[1,3,2,64,128]{4,3,2,1,0:T(8,128)}, f32[1,2,64,128]{3,2,1,0:T(8,128)}, f32[1,3,2,64,128]{4,3,2,1,0:T(8,128)}) custom-call(f32[1,2,64,128]{3,2,1,0:T(8,128)S(1)} %get-tuple-element.8.refs_0_, f32[1,3,2,64,128]{4,3,2,1,0:T(8,128)S(1)} %get-tuple-element.9.refs_1_, ...), custom_call_target="tpu_custom_call" | custom-call | bytes 1000000 | tf_op jit(solution)/shard_map/pallas_call | solution.py:574
